TPU v7x, 128 devices: a whole 4x4x4 slice. The times are simulated.
128 devices in a mesh: row: 8 (over z_lo, x), col: 16 (over y, z_hi, core).
Axes of the slice: x: 4, y: 4, z: 4 (z_hi: 2, z_lo: 2; z = z_hi * 2 + z_lo), core: 2. Of those that a mesh axis runs over, the one named last changes fastest.
Arguments:
- three_centre: bfloat16 [64, 2048, 2048], P('row', 'col'), may hold values from -6 to 6
- green_virt: bfloat16 [2048, 2048], P(('row', 'col')), may hold values from -0.25 to 0.25
- green_occ: bfloat16 [2048, 2048], P(('row', 'col')), may hold values from -0.25 to 0.25
- pattern: int32 [64, 64], replicated, may hold values 0 or 1
- block_sizes: int32 [64], replicated, may hold values from 8 to 32
- atom_order: int32 [64], replicated, may hold values from 0 to 63, each once
Outputs:
- projected: bfloat16 [2048, 64, 2048], P('row', None, 'col')
Inputs may be any that keep to these rules, and one draw needn't show every extreme that they name: `atom_order`: each atom index appears exactly once.
All inputs are finite; a program needn't handle non-finite values.
Results may differ from a plain program's by a relative error of at most 0.0049.
Values may be sent and summed in bfloat16 or wider, within the bound.
A program may use at most 128 MiB of HBM per device.

v0:
```python
import jax
import jax.numpy as jnp
from jax import lax
from jax.sharding import PartitionSpec as P

BLK = 32


def order_columns(atom_order):
    slot_ids = jnp.arange(BLK, dtype=jnp.int32)
    return (atom_order[:, None] * BLK + slot_ids[None, :]).reshape(-1)


def green_rows(matrix, folder, initial):
    return folder(initial, lax.all_gather(matrix, ("row", "col"), axis=0, tiled=True), jnp.int32(0))


def per_device(three_centre, green_virt, green_occ, pattern, block_sizes, atom_order):
    slab_rows, own_cols, orbitals = three_centre.shape
    atoms_here = own_cols // BLK
    column = lax.axis_index("col")
    usable = (
        lax.broadcasted_iota(jnp.int32, (block_sizes.shape[0], BLK), 1) < block_sizes[:, None]
    ).reshape(-1)
    own_usable = lax.dynamic_slice_in_dim(usable, column * own_cols, own_cols, 0)
    own_pattern = lax.dynamic_slice_in_dim(pattern, column * atoms_here, atoms_here, 0)
    paired = jnp.repeat(jnp.repeat(own_pattern > 0, BLK, axis=0), BLK, axis=1)
    kept_mask = paired & own_usable[:, None] & usable[None, :]
    filtered = jnp.where(kept_mask[None], three_centre, jnp.zeros((), three_centre.dtype))
    flattened = filtered.reshape(slab_rows * own_cols, orbitals)
    columns_order = order_columns(atom_order)

    def first_fold(running, shard_rows, offset):
        return jnp.dot(flattened, shard_rows, preferred_element_type=jnp.float32)

    initial = jnp.zeros((slab_rows * own_cols, orbitals), jnp.float32)
    summed = green_rows(green_virt, first_fold, initial)
    half_done = summed.astype(jnp.bfloat16)
    half_done = jnp.take(half_done, columns_order, axis=1)
    half_done = half_done.reshape(slab_rows, own_cols, orbitals)
    exchanged = lax.all_to_all(half_done, "col", split_axis=2, concat_axis=1, tiled=True)

    def second_fold(running, shard_rows, offset):
        return jnp.einsum("mk,pmc->kpc", shard_rows, exchanged, preferred_element_type=jnp.float32)

    second = green_rows(
        green_occ, second_fold, jnp.zeros((orbitals, slab_rows, exchanged.shape[2]), jnp.float32)
    )
    return lax.all_to_all(
        second.astype(jnp.bfloat16), "row", split_axis=0, concat_axis=1, tiled=True
    )


def solution(mesh):
    in_specs = (
        P("row", "col", None),
        P(("row", "col"), None),
        P(("row", "col"), None),
        P(),
        P(),
        P(),
    )
    out_specs = P("row", None, "col")
    return jax.shard_map(
        per_device, mesh=mesh, in_specs=in_specs, out_specs=out_specs, check_vma=False
    )
```

profile of v0, /device:TPU:0, one launch (start us, length us, event | category | flops | bytes accessed | tf_op | source)
XLA Modules:
  0.0 541.3 jit_solution(564335626811392272)
XLA Ops:
  6.5 0.0 all-gather.3.cloned.1.call-start
  6.5 0.7 all-gather.3.cloned.1.call-update
  7.3 0.0 all-gather.5.cloned.1.call-start
  7.3 0.7 all-gather.5.cloned.1.call-update
  8.0 0.7 broadcast_multiply_fusion
  8.7 0.1 iota_add_fusion
  8.7 0.1 add.67
  8.8 0.1 add.61
  8.9 0.7 iota_compare_fusion
  9.6 0.1 lt.48
  9.7 0.7 dynamic-slice_compare_fusion
  10.4 0.1 copy.21
  10.5 0.1 dynamic_slice.7
  10.6 0.3 fusion.4
  11.0 0.4 copy.22
  11.4 5.1 broadcast_select_fusion
  16.5 198.3 %all-gather.3.cloned.1.call-done = bf16[2048,2048]{1,0:T(8,128)(2,1)} async-done(((bf16[16,2048]{1,0:T(8,128)(2,1)}), bf16[2048,2048]{1,0:T(8,128)(2,1)}) %all-gather.3.cloned.1.call-update) | async-done | bytes 8388624 | tf_op jit(solution)/shard_map/all_gather | solution.py:15
  214.9 13.8 %convolution_convert_fusion = bf16[1024,2048]{1,0:T(8,128)(2,1)} fusion(bf16[1024,2048]{1,0:T(8,128)(2,1)} %bitcast.39, bf16[2048,2048]{1,0:T(8,128)(2,1)} %all-gather.3.cloned.1.call-done), kind=kOutput, calls=%fused_computation.7 | convolution fusion | flops 8592031744 | bytes 16777216 | tf_op jit(solution)/shard_map/dot_general | solution.py:34
  228.7 6.4 %copy.23 = bf16[1024,2048]{0,1:T(8,128)(2,1)} copy(bf16[1024,2048]{1,0:T(8,128)(2,1)} %convolution_convert_fusion) | data formatting | bytes 8388608 | tf_op jit(solution)/shard_map/convert_element_type | solution.py:38
  235.1 13.7 %gather_fusion = bf16[2048,1024]{1,0:T(8,128)(2,1)} fusion(bf16[1024,2048]{0,1:T(8,128)(2,1)} %copy.23, s32[2048]{0:T(1024)S(1)} %broadcast_clamp_fusion), kind=kCustom, calls=%fused_computation | custom fusion | bytes 8396800 | tf_op jit(solution)/shard_map/jit(_take)/gather | solution.py:39
  248.7 3.3 copy.29
  252.0 7.5 %bitcast_select_fusion = bf16[8,128,2048]{1,0,2:T(8,128)(2,1)S(1)} fusion(bf16[256,8,8,128]{3,2,1,0:T(8,128)(2,1)S(1)} %copy.29, pred[2048]{0:T(1024)(128)(4,1)S(1)} %compare_and_fusion), kind=kLoop, calls=%fused_computation.3 | loop fusion | flops 2097152 | bytes 8390656 | tf_op jit(solution)/shard_map/jit(_take)/select_n | solution.py:39
  259.5 64.2 %all_to_all.36 = bf16[8,128,2048]{1,0,2:T(8,128)(2,1)S(1)} all-to-all(bf16[8,128,2048]{1,0,2:T(8,128)(2,1)S(1)} %bitcast_select_fusion), channel_id=1, replica_groups=mesh['row'=8,'col'=16] {'col'}, dimensions={2} | all-to-all | bytes 8388608 | tf_op jit(solution)/shard_map/all_to_all | solution.py:41
  323.7 4.7 copy.25
  328.4 7.3 %all_to_all.29 = bf16[8,2048,128]{1,2,0:T(8,128)(2,1)} reshape(bf16[8,16,128,128]{2,1,3,0:T(8,128)(2,1)} %copy.25) | data formatting | bytes 8388608 | tf_op jit(solution)/shard_map/all_to_all | solution.py:41
  335.7 121.7 %all-gather.5.cloned.1.call-done = bf16[2048,2048]{1,0:T(8,128)(2,1)} async-done(((bf16[16,2048]{1,0:T(8,128)(2,1)}), bf16[2048,2048]{1,0:T(8,128)(2,1)}) %all-gather.5.cloned.1.call-update) | async-done | bytes 8388624 | tf_op jit(solution)/shard_map/all_gather | solution.py:15
  457.4 13.8 %convert_bitcast_fusion = bf16[2048,8,128]{0,2,1:T(8,128)(2,1)} fusion(bf16[8,2048,128]{1,2,0:T(8,128)(2,1)} %all_to_all.29, bf16[2048,2048]{1,0:T(8,128)(2,1)} %all-gather.5.cloned.1.call-done), kind=kOutput, calls=%fused_computation.5 | convolution fusion | flops 8592031744 | bytes 16777216 | tf_op jit(solution)/shard_map/mk,pmc->kpc/dot_general | solution.py:44
  471.2 6.7 %copy.26 = bf16[2048,8,128]{2,1,0:T(8,128)(2,1)} copy(bf16[2048,8,128]{0,2,1:T(8,128)(2,1)} %convert_bitcast_fusion) | data formatting | bytes 8388608 | tf_op jit(solution)/shard_map/convert_element_type | solution.py:50
  477.9 53.3 %all_to_all.37 = bf16[2048,8,128]{2,1,0:T(8,128)(2,1)S(1)} all-to-all(bf16[2048,8,128]{2,1,0:T(8,128)(2,1)} %copy.26), channel_id=1, replica_groups=mesh['row'=8,'col'=16] {'row'}, dimensions={0} | all-to-all | bytes 8388608 | tf_op jit(solution)/shard_map/all_to_all | solution.py:49
  531.2 3.2 copy.31
  (4 shorter events, 0.0 us)
Async XLA Ops:
  6.5 208.3 %all-gather.3.cloned.1.call-start = ((), (), s32[]{:S(2)}) async-start(), calls=%async_computation.2 | async-start | bytes 8454144 | tf_op jit(solution)/shard_map/all_gather | solution.py:15
  7.3 450.1 %all-gather.5.cloned.1.call-start = ((), (), s32[]{:S(2)}) async-start(), calls=%async_computation.3 | async-start | bytes 8454144 | tf_op jit(solution)/shard_map/all_gather | solution.py:15
Sparse Core Ops, SparseCore 0:
  9.1 205.7 all-gather.2
  216.6 240.7 all-gather.4
where the time goes:
time: 542 us; the launch traced here: 541 us
  waiting for transfers between devices  321 us (59%)
  blocking collectives  117 us (22%)
  local copies, waits for them, and re-layouts  46.2 us (9%)
  matrix products  27.6 us (5%)
  other arithmetic  15.1 us (3%)
  between operations  13.5 us (2%)
    all_gather x2, waiting for transfers between devices, green_rows(): lax.all_gather(matrix, ('row', 'col'), axis=0, tiled=True)  320 us
    all_to_all x1, blocking collectives, per_device(): lax.all_to_all(half_done, 'col', split_axis=2, concat_axis=1, tiled=True)  64.2 us
    all_to_all x1, blocking collectives, per_device(): lax.all_to_all(second.astype(jnp.bfloat16), 'row', split_axis=0, concat_a...  53.3 us
    dot_general x1, matrix products, first_fold(): return jnp.dot(flattened, shard_rows, preferred_element_type=jnp.float32)  13.8 us
    dot_general x1, matrix products, second_fold(): jnp.einsum('mk,pmc->kpc', shard_rows, exchanged, preferred_element_type=j...  13.8 us
    gather x1, local copies, waits for them, and re-layouts, per_device(): half_done = jnp.take(half_done, columns_order, axis=1)  13.7 us
    all_to_all x2, local copies, waits for them, and re-layouts, per_device(): lax.all_to_all(half_done, 'col', split_axis=2, concat_axis=1, tiled=True)  12 us
  transfers between devices with their start and end apart: 2, of which 2 were waited for; matrix products, arithmetic and copies ran while one was open for 11% of the time, Pallas kernels for 0%

commit v1 on v0

v1 whole, which is shorter than its diff:
```python
import jax
import jax.numpy as jnp
from jax import lax
from jax.experimental import pallas as pl
from jax.experimental.pallas import tpu as pltpu
from jax.sharding import PartitionSpec as P

MESH = pl.DeviceIdType.MESH
BF = jnp.bfloat16
F32 = jnp.float32
NC = 4
PARTS = ((0, 3), (3, 3), (6, 2))
ORDERS = ("xyz", "yzx", "zxy")


def me():
    r = lax.axis_index("row")
    c = lax.axis_index("col")
    return {
        "x": lax.rem(r, 4),
        "y": c // 4,
        "z": lax.rem(c // 2, 2) * 2 + r // 4,
        "k": lax.rem(c, 2),
    }


def device(p):
    return {"row": lax.rem(p["z"], 2) * 4 + p["x"], "col": (p["y"] * 2 + p["z"] // 2) * 2 + p["k"]}


def moved(p, **by):
    q = dict(p)
    for axis, d in by.items():
        q[axis] = lax.rem(p[axis] + d, 2) if axis == "k" else lax.rem(p[axis] + d + 4, 4)
    return q


def flip(p, axis):
    q = dict(p)
    q[axis] = p[axis] + 1 - 2 * lax.rem(p[axis], 2)
    return q


def partners(p):
    found = []
    for axis in "xyz":
        for d in (1, 2, 3):
            for e in (0, 1):
                found.append(moved(p, **{axis: d, "k": e}))
    found.append(moved(p, k=1))
    for d in (1, 2, 3):
        found.append(moved(p, y=d, z=2))
        found.append(flip(moved(p, x=d), "z"))
    found.append(flip(moved(p, z=2, k=1), "y"))
    found.append(flip(moved(p, y=2), "z"))
    return found


def kernel(gv, go, order, sizes, pattern, t_hbm, out,
           turned, gp, gvb, t2, mask, hs, hr, gst, got, ss,
           t_sem, own_sem, ts_sem, tr_sem, v1s, v1r, v2s, v2r, v3s, v3r,
           o1s, o1r, o2s, o2r, o3s, o3r, o4s, o4r, hss, hrs, hl, sss, srs, sl):
    p = me()
    x, y, z, k = p["x"], p["y"], p["z"], p["k"]
    zl, zh, yl, yh = lax.rem(z, 2), z // 2, lax.rem(y, 2), y // 2
    row, col = lax.axis_index("row"), lax.axis_index("col")

    def remote(src, dst, send, recv, to):
        return pltpu.make_async_remote_copy(
            src_ref=src, dst_ref=dst, send_sem=send, recv_sem=recv, device_id=device(to), device_id_type=MESH
        )

    def t_load(c):
        two = pl.ds(c * 2, 2)
        return pltpu.make_async_copy(t_hbm.at[two], t2.at[two, k], t_sem.at[c])

    for c in range(NC):
        t_load(c).start()

    barrier = pltpu.get_barrier_semaphore()
    peers = partners(p)
    for q in peers:
        pl.semaphore_signal(barrier, inc=1, device_id=device(q), device_id_type=MESH)

    lane_slot = lax.broadcasted_iota(jnp.int32, (16, 128), 1) // 32
    for b in range(16):
        source = gv[:, b * 128:(b + 1) * 128].astype(F32)
        for t in range(4):
            turned[t, b] = pltpu.roll(source, t * 32, 1) if t else source

    def permute(j, carry):
        wanted = jnp.zeros((16, 128), jnp.int32)
        for s in range(4):
            wanted = jnp.where(lane_slot == s, order[4 * j + s], wanted)
        block = jnp.zeros((16, 128), F32)
        for t in range(4):
            first_atom = wanted - lax.rem(lane_slot - t + 4, 4)
            for b in range(16):
                block = jnp.where(first_atom == 4 * b, turned[t, b], block)
        gp[lax.rem(j, 2), j // 2] = block.astype(BF)
        return carry

    lax.fori_loop(0, 16, permute, 0)

    def rows16(core):
        return pl.ds(pl.multiple_of(core * 16, 16), 16)

    own = pltpu.make_async_copy(gp.at[k], gvb.at[:, zl, x, y, zh, rows16(k)], own_sem.at[0])
    own.start()
    own_o = pltpu.make_async_copy(
        go.at[:, pl.ds(pl.multiple_of(k * 1024, 1024), 1024)], gst.at[yl * 4 + zh * 2 + k], own_sem.at[1]
    )
    own_o.start()

    pl.semaphore_wait(barrier, len(peers))

    def v1(part, d, e, mine):
        k0, nk = PARTS[part]
        axis = ORDERS[part][0]
        to = moved(p, **{axis: d, "k": e})
        frm = p if mine else moved(p, **{axis: -d, "k": e})
        dst = gvb.at[pl.ds(k0, nk), lax.rem(frm["z"], 2), frm["x"], frm["y"], frm["z"] // 2, rows16(frm["k"])]
        return remote(gp.at[to["k"], pl.ds(k0, nk)], dst, v1s.at[part, d - 1, e], v1r.at[part, d - 1, e], to)

    def v1_sibling(mine):
        frm = p if mine else moved(p, k=1)
        return remote(
            gp.at[1 - k], gvb.at[:, zl, x, y, zh, rows16(frm["k"])], v1s.at[3, 0, 0], v1r.at[3, 0, 0], moved(p, k=1)
        )

    v1_sibling(True).start()
    for d in (1, 3, 2):
        for part in range(3):
            for e in (0, 1):
                v1(part, d, e, True).start()

    def o1(a, b, e, mine):
        to = moved(p, z=2 * b, k=e)
        if a:
            to = flip(to, "y")
        frm = p if mine else to
        half = pl.ds(pl.multiple_of(to["k"] * 1024, 1024), 1024)
        slot = lax.rem(frm["y"], 2) * 4 + (frm["z"] // 2) * 2 + frm["k"]
        return remote(go.at[:, half], gst.at[slot], o1s.at[a, b, e], o1r.at[a, b, e], to)

    group = [(a, b, e) for a in (0, 1) for b in (0, 1) for e in (0, 1) if a or b or e]
    for abe in group:
        o1(*abe, True).start()

    atom_of_row = lax.broadcasted_iota(jnp.int32, (128, 64), 0) // 32 + col * 4
    pick = (lax.broadcasted_iota(jnp.int32, (128, 64), 1) == atom_of_row).astype(F32)
    spread = (
        lax.broadcasted_iota(jnp.int32, (64, 2048), 1) // 32 == lax.broadcasted_iota(jnp.int32, (64, 2048), 0)
    ).astype(BF)
    size_row = sizes[...].astype(F32)
    own_size = jnp.sum(pick * size_row, axis=1, keepdims=True)
    row_ok = lax.rem(lax.broadcasted_iota(jnp.int32, (128, 1), 0), 32).astype(F32) < own_size
    paired = jnp.dot(pick.astype(BF), pattern[...].astype(F32).astype(BF), preferred_element_type=F32)
    paired = jnp.where(row_ok, paired, 0.0)
    paired = jnp.dot(paired.astype(BF), spread, preferred_element_type=F32)
    all_sizes = jnp.dot(jnp.broadcast_to(size_row, (8, 64)).astype(BF), spread, preferred_element_type=F32)[0:1]
    column_ok = lax.rem(lax.broadcasted_iota(jnp.int32, (1, 2048), 1), 32).astype(F32) < all_sizes
    mask[...] = jnp.where(column_ok, paired, 0.0).astype(BF)

    def t_share(c, mine):
        part = t2.at[pl.ds(c * 2, 2), k if mine else 1 - k]
        return remote(part, part, ts_sem.at[c], tr_sem.at[c], moved(p, k=1))

    def filter_chunk(c, carry):
        t_load(c).wait()

        def strip(i, inner):
            rows = pl.ds(pl.multiple_of(i * 16, 16), 16)
            m = mask[rows, :]
            for q in range(2):
                t2[c * 2 + q, k, rows, :] = t2[c * 2 + q, k, rows, :] * m
            return inner

        lax.fori_loop(0, 8, strip, 0)
        t_share(c, True).start()
        return carry

    lax.fori_loop(0, NC, filter_chunk, 0)

    def v_slot(part, at, full):
        k0, nk = PARTS[part]
        every = slice(None)
        return gvb.at[
            pl.ds(k0, nk),
            every if "z" in full else lax.rem(at["z"], 2),
            every if "x" in full else at["x"],
            every if "y" in full else at["y"],
            every if "z" in full else at["z"] // 2,
        ]

    def v23(step, part, d, mine):
        axis = ORDERS[part][step]
        slot = v_slot(part, p if mine else moved(p, **{axis: -d}), ORDERS[part][:step])
        s, r = ((v2s, v2r), (v3s, v3r))[step - 1]
        return remote(slot, slot, s.at[part, d - 1], r.at[part, d - 1], moved(p, **{axis: d}))

    own.wait()
    v1_sibling(False).wait_recv()
    for part in range(3):
        for d in (1, 2, 3):
            for e in (0, 1):
                v1(part, d, e, False).wait_recv()
        for d in (1, 3, 2):
            v23(1, part, d, True).start()

    own_o.wait()
    for abe in group:
        o1(*abe, False).wait_recv()
    got[zl, x, yh, k] = gst[...].reshape(128, 1024).T

    def o2(a, b, mine):
        to = moved(p, y=2 * a)
        if b:
            to = flip(to, "z")
        frm = p if mine else to
        slot = got.at[lax.rem(frm["z"], 2), x, frm["y"] // 2, k]
        return remote(slot, slot, o2s.at[a, b], o2r.at[a, b], to)

    for part in range(3):
        for d in (1, 2, 3):
            v23(1, part, d, False).wait_recv()
        for d in (1, 3, 2):
            v23(2, part, d, True).start()

    trio = ((0, 1), (1, 0), (1, 1))
    for ab in trio:
        o2(*ab, True).start()

    def o3(d, mine):
        slot = got.at[:, x if mine else moved(p, x=-d)["x"], :, k]
        return remote(slot, slot, o3s.at[d - 1], o3r.at[d - 1], moved(p, x=d))

    def o4(d, mine):
        slot = got.at[:, moved(p, x=-d)["x"], :, k if mine else 1 - k]
        return remote(slot, slot, o4s.at[d], o4r.at[d], moved(p, k=1))

    for ab in trio:
        o2(*ab, False).wait_recv()
    for d in (1, 3, 2):
        o3(d, True).start()
    o4(0, True).start()

    for c in range(NC):
        t_share(c, False).wait_recv()
    for part in range(3):
        for d in (1, 2, 3):
            v23(2, part, d, False).wait_recv()

    def h_copy(c, s, e, mine):
        to = moved(p, y=s, z=2 * e)
        frm = p if mine else moved(p, y=-s, z=2 * e)
        return remote(
            hs.at[c, to["y"] * 2 + to["z"] // 2],
            hr.at[c, :, frm["y"] * 2 + frm["z"] // 2],
            hss.at[c, s, e], hrs.at[c, s, e], to,
        )

    def h_own(c):
        chip = y * 2 + zh
        return pltpu.make_async_copy(hs.at[c, chip], hr.at[c, :, chip], hl.at[c])

    def first(i, carry):
        c, s = i // 4, lax.rem(i, 4)
        pair = lax.rem(y + s, 4) * 2
        rhs = jnp.concatenate([gvb[pair + q].reshape(2048, 128) for q in range(2)], axis=1)
        lhs = t2[pl.ds(c * 2, 2)].reshape(512, 2048)
        h = jnp.dot(lhs, rhs, preferred_element_type=F32).astype(BF)
        for q in range(2):
            hs[c, pair + q] = h[:, q * 128:(q + 1) * 128].reshape(2, 256, 128)
        h_copy(c, s, 1, True).start()

        @pl.when(s == 0)
        def _():
            h_own(c).start()

        @pl.when(s > 0)
        def _():
            h_copy(c, s, 0, True).start()

        return carry

    lax.fori_loop(0, NC * 4, first, 0)

    for d in (1, 3, 2):
        o3(d, False).wait_recv()
        o4(d, True).start()
    for d in range(4):
        o4(d, False).wait_recv()

    def s_copy(c, d, e, mine):
        to = moved(p, x=d)
        frm = p if mine else moved(p, x=-d)
        if e:
            to = flip(to, "z")
            if not mine:
                frm = flip(frm, "z")
        frm_row = lax.rem(frm["z"], 2) * 4 + frm["x"]
        return remote(ss.at[c, d, e], out.at[pl.ds(frm_row * 8 + c * 2, 2)], sss.at[c, d, e], srs.at[c, d, e], to)

    def s_own(c):
        return pltpu.make_async_copy(ss.at[c, 0, 0], out.at[pl.ds(row * 8 + c * 2, 2)], sl.at[c])

    def second(c, carry):
        h_own(c).wait()
        h_copy(c, 0, 1, False).wait_recv()
        for s in (1, 2, 3):
            for e in (0, 1):
                h_copy(c, s, e, False).wait_recv()

        def tile(d, inner):
            rows = pl.ds(pl.multiple_of(lax.rem(x + d, 4) * 256, 256), 256)
            lhs = jnp.concatenate(
                [
                    jnp.concatenate(
                        [
                            got[b // 8, lax.rem(b // 2, 4), lax.rem(b, 2), zl if e == 0 else 1 - zl, rows, :]
                            for b in range(16)
                        ],
                        axis=1,
                    )
                    for e in (0, 1)
                ],
                axis=0,
            )
            rhs = jnp.concatenate([hr[c, q].reshape(2048, 128) for q in range(2)], axis=1)
            r = jnp.dot(lhs, rhs, preferred_element_type=F32).astype(BF)
            for e in (0, 1):
                for q in range(2):
                    ss[c, d, e, q] = r[e * 256:(e + 1) * 256, q * 128:(q + 1) * 128]
            s_copy(c, d, 1, True).start()

            @pl.when(d == 0)
            def _():
                s_own(c).start()

            @pl.when(d > 0)
            def _():
                s_copy(c, d, 0, True).start()

            return inner

        lax.fori_loop(0, 4, tile, 0)
        return carry

    lax.fori_loop(0, NC, second, 0)

    v1_sibling(True).wait_send()
    for part in range(3):
        for d in (1, 2, 3):
            for e in (0, 1):
                v1(part, d, e, True).wait_send()
            v23(1, part, d, True).wait_send()
            v23(2, part, d, True).wait_send()
    for abe in group:
        o1(*abe, True).wait_send()
    for ab in trio:
        o2(*ab, True).wait_send()
    for d in (1, 2, 3):
        o3(d, True).wait_send()
    for d in range(4):
        o4(d, True).wait_send()

    def drain(c, carry):
        t_share(c, True).wait_send()
        s_own(c).wait()
        for s in range(4):
            for e in (0, 1):
                if s or e:
                    h_copy(c, s, e, True).wait_send()
                    s_copy(c, s, e, True).wait_send()
                    s_copy(c, s, e, False).wait_recv()
        return carry

    lax.fori_loop(0, NC, drain, 0)


def per_device(three_centre, green_virt, green_occ, pattern, block_sizes, atom_order):
    vmem = pl.BlockSpec(memory_space=pltpu.VMEM)
    dma = pltpu.SemaphoreType.DMA
    blocks = pl.pallas_call(
        kernel,
        out_shape=jax.ShapeDtypeStruct((64, 256, 128), BF),
        in_specs=[vmem, vmem, pl.BlockSpec(memory_space=pltpu.SMEM), vmem, vmem, pl.BlockSpec(memory_space=pl.ANY)],
        out_specs=pl.BlockSpec(memory_space=pl.ANY),
        scratch_shapes=[
            pltpu.VMEM((4, 16, 16, 128), F32),
            pltpu.VMEM((2, 8, 16, 128), BF),
            pltpu.VMEM((8, 2, 4, 4, 2, 32, 128), BF),
            pltpu.VMEM((8, 2, 128, 2048), BF),
            pltpu.VMEM((128, 2048), BF),
            pltpu.VMEM((NC, 8, 2, 256, 128), BF),
            pltpu.VMEM((NC, 2, 8, 256, 128), BF),
            pltpu.VMEM((8, 16, 1024), BF),
            pltpu.VMEM((2, 4, 2, 2, 1024, 128), BF),
            pltpu.VMEM((NC, 4, 2, 2, 256, 128), BF),
            dma((NC,)), dma((2,)), dma((NC,)), dma((NC,)),
            dma((4, 3, 2)), dma((4, 3, 2)), dma((3, 3)), dma((3, 3)), dma((3, 3)), dma((3, 3)),
            dma((2, 2, 2)), dma((2, 2, 2)), dma((2, 2)), dma((2, 2)), dma((3,)), dma((3,)), dma((4,)), dma((4,)),
            dma((NC, 4, 2)), dma((NC, 4, 2)), dma((NC,)), dma((NC, 4, 2)), dma((NC, 4, 2)), dma((NC,)),
        ],
        compiler_params=pltpu.CompilerParams(
            collective_id=0, has_side_effects=True, vmem_limit_bytes=56 * 2**20
        ),
        name="contract",
    )(green_virt, green_occ, atom_order, block_sizes.reshape(1, -1), pattern, three_centre)
    return jnp.transpose(blocks, (1, 0, 2))


def solution(mesh):
    in_specs = (P("row", "col", None), P(("row", "col"), None), P(("row", "col"), None), P(), P(), P())
    return jax.shard_map(
        per_device, mesh=mesh, in_specs=in_specs, out_specs=P("row", None, "col"), check_vma=False
    )
```

time: 542 us -> 158 us (0.29)
  the two profiles are of different devices: /device:TPU:0 before, /device:TPU:21 now
where the time goes in v1:
time: 158 us; the launch traced here: 157 us
  Pallas kernels  151 us (96%)
  local copies, waits for them, and re-layouts  6.9 us (4%)
    pallas_call x1, Pallas kernels, per_device(): pl.pallas_call(kernel, out_shape=jax.ShapeDtypeStruct((64, 256, 128), BF)...  151 us
    transpose x1, local copies, waits for them, and re-layouts, per_device(): return jnp.transpose(blocks, (1, 0, 2))  6.9 us

profile of v1, /device:TPU:21, one launch (start us, length us, event | category | flops | bytes accessed | tf_op | source)
XLA Modules:
  0.0 157.5 jit_solution(3026411172959978200)
XLA Ops:
  0.0 150.6 %contract.1 = bf16[64,256,128]{2,1,0:T(8,128)(2,1)} custom-call(bf16[16,2048]{1,0:T(8,128)(2,1)} %gv.1, bf16[16,2048]{1,0:T(8,128)(2,1)} %go.1, s32[64]{0:T(128)} %order.1, s32[1,64]{1,0:T(1,128)} %bitcast.3, s32[64,64]{1,0:T(8,128)} %pattern.1, bf16[8,128,2048]{2,1,0:T(8,128)(2,1)} %t_hbm.1), custom_call_target="tpu_custom_call" | custom-call | tf_op jit(solution)/shard_map/contract/pallas_call | solution.py:385
  150.6 6.9 %copy.7 = bf16[256,64,128]{2,1,0:T(8,128)(2,1)} copy(bf16[256,64,128]{2,0,1:T(8,128)(2,1)} %bitcast.2) | data formatting | bytes 8388608 | tf_op jit(solution)/shard_map/transpose | solution.py:411

commit v2 on v1

v2 whole, which is shorter than its diff:
```python
import jax
import jax.numpy as jnp
from jax import lax
from jax.experimental import pallas as pl
from jax.experimental.pallas import tpu as pltpu
from jax.sharding import PartitionSpec as P

MESH = pl.DeviceIdType.MESH
BF = jnp.bfloat16
F32 = jnp.float32
NC = 4
ORDERS = ("yzx", "zxy")


def me():
    r = lax.axis_index("row")
    c = lax.axis_index("col")
    return {
        "x": lax.rem(r, 4),
        "y": c // 4,
        "z": lax.rem(c // 2, 2) * 2 + r // 4,
        "k": lax.rem(c, 2),
    }


def turn(i):
    return i + (i // 2) * (5 - 2 * i)


def device(p):
    return {"row": lax.rem(p["z"], 2) * 4 + p["x"], "col": (p["y"] * 2 + p["z"] // 2) * 2 + p["k"]}


def moved(p, **by):
    q = dict(p)
    for axis, d in by.items():
        q[axis] = lax.rem(p[axis] + d, 2) if axis == "k" else lax.rem(p[axis] + d + 4, 4)
    return q


def flip(p, axis):
    q = dict(p)
    q[axis] = p[axis] + 1 - 2 * lax.rem(p[axis], 2)
    return q


def partners(p):
    found = [moved(p, k=1)]
    for d in (1, 2, 3):
        for e in (0, 1):
            found.append(moved(p, y=d, k=e))
            found.append(moved(p, z=d, k=e))
        found.append(moved(p, x=d))
        found.append(moved(p, y=d, z=2))
        found.append(flip(moved(p, x=d), "z"))
    return found


def kernel(gv, go, order, sizes, pattern, t_hbm, out,
           turned, gp, gvb, t2, mask, hs, hr, gst, got, ss,
           t_sem, own_sem, ts_sem, tr_sem, v1s, v1r, v2s, v2r, vys, vyr, vxs, vxr,
           o1s, o1r, o2s, o2r, o3s, o3r, o4s, o4r, hss, hrs, hl, sss, srs, sl):
    p = me()
    x, y, z, k = p["x"], p["y"], p["z"], p["k"]
    zl, zh, yl, yh = lax.rem(z, 2), z // 2, lax.rem(y, 2), y // 2
    row, col = lax.axis_index("row"), lax.axis_index("col")

    def remote(src, dst, send, recv, to):
        return pltpu.make_async_remote_copy(
            src_ref=src, dst_ref=dst, send_sem=send, recv_sem=recv, device_id=device(to), device_id_type=MESH
        )

    def t_load(c):
        two = pl.ds(c * 2, 2)
        return pltpu.make_async_copy(t_hbm.at[two], t2.at[two, k], t_sem.at[c])

    for c in range(NC):
        t_load(c).start()

    barrier = pltpu.get_barrier_semaphore()
    peers = partners(p)
    for q in peers:
        pl.semaphore_signal(barrier, inc=1, device_id=device(q), device_id_type=MESH)

    lane_slot = lax.broadcasted_iota(jnp.int32, (16, 128), 1) // 32
    for b in range(16):
        source = gv[:, b * 128:(b + 1) * 128].astype(F32)
        for t in range(4):
            turned[t, b] = pltpu.roll(source, t * 32, 1) if t else source

    def permute(j, carry):
        wanted = jnp.zeros((16, 128), jnp.int32)
        for s in range(4):
            wanted = jnp.where(lane_slot == s, order[4 * j + s], wanted)
        block = jnp.zeros((16, 128), F32)
        for t in range(4):
            first_atom = wanted - lax.rem(lane_slot - t + 4, 4)
            for b in range(16):
                block = jnp.where(first_atom == 4 * b, turned[t, b], block)
        gp[lax.rem(j, 2), lax.rem(j // 2, 2), j // 4] = block.astype(BF)
        return carry

    lax.fori_loop(0, 16, permute, 0)

    def rows16(core):
        return pl.ds(pl.multiple_of(core * 16, 16), 16)

    own = pltpu.make_async_copy(gp.at[k], gvb.at[:, :, zl, x, y, zh, rows16(k)], own_sem.at[0])
    own.start()
    own_o = pltpu.make_async_copy(
        go.at[:, pl.ds(pl.multiple_of(k * 1024, 1024), 1024)], gst.at[y * 2 + k], own_sem.at[1]
    )
    own_o.start()

    pl.semaphore_wait(barrier, len(peers))

    def v1(part, d, e, mine):
        axis = ORDERS[part][0]
        to = moved(p, **{axis: d, "k": e})
        frm = p if mine else moved(p, **{axis: -d, "k": e})
        dst = gvb.at[part, :, lax.rem(frm["z"], 2), frm["x"], frm["y"], frm["z"] // 2, rows16(frm["k"])]
        return remote(gp.at[to["k"], part], dst, v1s.at[part, d - 1, e], v1r.at[part, d - 1, e], to)

    def v1_sibling(mine):
        frm = p if mine else moved(p, k=1)
        return remote(
            gp.at[1 - k], gvb.at[:, :, zl, x, y, zh, rows16(frm["k"])], v1s.at[2, 0, 0], v1r.at[2, 0, 0], moved(p, k=1)
        )

    v1_sibling(True).start()
    for d in (1, 3, 2):
        for part in (0, 1):
            for e in (0, 1):
                v1(part, d, e, True).start()

    def o1(d, e, mine):
        to = moved(p, y=d, k=e)
        frm = p if mine else moved(p, y=-d, k=e)
        half = pl.ds(pl.multiple_of(to["k"] * 1024, 1024), 1024)
        return remote(go.at[:, half], gst.at[frm["y"] * 2 + frm["k"]], o1s.at[d, e], o1r.at[d, e], to)

    group = [(d, e) for d in range(4) for e in (0, 1) if d or e]
    for de in group:
        o1(*de, True).start()

    atom_of_row = lax.broadcasted_iota(jnp.int32, (128, 64), 0) // 32 + col * 4
    pick = (lax.broadcasted_iota(jnp.int32, (128, 64), 1) == atom_of_row).astype(F32)
    spread = (
        lax.broadcasted_iota(jnp.int32, (64, 2048), 1) // 32 == lax.broadcasted_iota(jnp.int32, (64, 2048), 0)
    ).astype(BF)
    size_row = sizes[...].astype(F32)
    own_size = jnp.sum(pick * size_row, axis=1, keepdims=True)
    row_ok = lax.rem(lax.broadcasted_iota(jnp.int32, (128, 1), 0), 32).astype(F32) < own_size
    paired = jnp.dot(pick.astype(BF), pattern[...].astype(F32).astype(BF), preferred_element_type=F32)
    paired = jnp.where(row_ok, paired, 0.0)
    paired = jnp.dot(paired.astype(BF), spread, preferred_element_type=F32)
    all_sizes = jnp.dot(jnp.broadcast_to(size_row, (8, 64)).astype(BF), spread, preferred_element_type=F32)[0:1]
    column_ok = lax.rem(lax.broadcasted_iota(jnp.int32, (1, 2048), 1), 32).astype(F32) < all_sizes
    mask[...] = jnp.where(column_ok, paired, 0.0).astype(BF)

    def t_share(c, mine):
        part = t2.at[pl.ds(c * 2, 2), k if mine else 1 - k]
        return remote(part, part, ts_sem.at[c], tr_sem.at[c], moved(p, k=1))

    def filter_chunk(c, carry):
        t_load(c).wait()

        def strip(i, inner):
            rows = pl.ds(pl.multiple_of(i * 16, 16), 16)
            m = mask[rows, :]
            for q in range(2):
                t2[c * 2 + q, k, rows, :] = t2[c * 2 + q, k, rows, :] * m
            return inner

        lax.fori_loop(0, 8, strip, 0)
        t_share(c, True).start()
        return carry

    lax.fori_loop(0, NC, filter_chunk, 0)

    def v2(part, d, mine):
        axis = ORDERS[part][1]
        at = p if mine else moved(p, **{axis: -d})
        azl, azh = lax.rem(at["z"], 2), at["z"] // 2
        slot = gvb.at[0, :, azl, x, :, azh] if part == 0 else gvb.at[1, :, :, at["x"], y, :]
        return remote(slot, slot, v2s.at[part, d - 1], v2r.at[part, d - 1], moved(p, **{axis: d}))

    own.wait()
    v1_sibling(False).wait_recv()
    for part in (0, 1):
        for d in (1, 2, 3):
            for e in (0, 1):
                v1(part, d, e, False).wait_recv()
        for d in (1, 3, 2):
            v2(part, d, True).start()

    own_o.wait()
    for de in group:
        o1(*de, False).wait_recv()
    got[zl, x, zh, k] = gst[...].reshape(128, 1024).T

    def o2(d, mine):
        at = p if mine else moved(p, z=-d)
        slot = got.at[lax.rem(at["z"], 2), x, at["z"] // 2, k]
        return remote(slot, slot, o2s.at[d - 1], o2r.at[d - 1], moved(p, z=d))

    for d in (1, 3, 2):
        o2(d, True).start()

    def vy(s, d, mine):
        pair = lax.rem((y + d if mine else y) + turn(s), 4)
        slot = gvb.at[1, pair, :, :, y if mine else moved(p, y=-d)["y"], :]
        return remote(slot, slot, vys.at[s, d - 1], vyr.at[s, d - 1], moved(p, y=d))

    def along_x(ref_of, send, recv, side, n, mine):
        step = 1 - 2 * side
        origin = (x if n < 2 else moved(p, x=-step)["x"]) if mine else moved(p, x=-step if n < 2 else 2)["x"]
        slot = ref_of(side if n == 2 else n, origin)
        return remote(slot, slot, send.at[side, n], recv.at[side, n], moved(p, x=step))

    def vx(s, side, n, mine):
        pair = lax.rem(y + turn(s), 4)
        return along_x(lambda half, at: gvb.at[0, pair, half, at], vxs.at[s], vxr.at[s], side, n, mine)

    def o3(t, side, n, mine):
        rows = pl.ds(t * 256, 256)
        return along_x(lambda half, at: got.at[half, at, :, k, rows], o3s.at[t], o3r.at[t], side, n, mine)

    def own_out(copy, i):
        for n in (0, 1):
            for side in (0, 1):
                copy(i, side, n if side == 0 else 1 - n, True).start()

    def pass_on(copy, i):
        for side in (0, 1):
            copy(i, side, side, False).wait_recv()
            copy(i, side, 2, True).start()

    def rest_in(copy, i):
        for side in (0, 1):
            copy(i, side, 1 - side, False).wait_recv()
            copy(i, side, 2, False).wait_recv()

    def o4(t, mine):
        slot = got.at[:, :, :, k if mine else 1 - k, pl.ds(t * 256, 256)]
        return remote(slot, slot, o4s.at[t], o4r.at[t], moved(p, k=1))

    for part in (0, 1):
        for d in (1, 2, 3):
            v2(part, d, False).wait_recv()

    own_out(vx, 0)
    own_out(vx, 1)

    def vy_start(s, carry):
        for d in (1, 3, 2):
            vy(s, d, True).start()
        return carry

    lax.fori_loop(0, 4, vy_start, 0)

    for c in range(NC):
        t_share(c, False).wait_recv()

    def h_copy(c, s, e, mine):
        to = moved(p, y=s, z=2 * e)
        frm = p if mine else moved(p, y=-s, z=2 * e)
        return remote(
            hs.at[c, to["y"] * 2 + to["z"] // 2],
            hr.at[c, :, frm["y"] * 2 + frm["z"] // 2],
            hss.at[c, s, e], hrs.at[c, s, e], to,
        )

    def h_own(c):
        chip = y * 2 + zh
        return pltpu.make_async_copy(hs.at[c, chip], hr.at[c, :, chip], hl.at[c])

    def first(i, carry):
        n, c = i // 4, lax.rem(i, 4)
        s = turn(n)

        @pl.when(i == 0)
        def _():
            for n in (0, 1):
                pass_on(vx, n)
                own_out(vx, n + 2)

        @pl.when(i == 4)
        def _():
            pass_on(vx, 2)

        @pl.when(i == 8)
        def _():
            pass_on(vx, 3)
            for d in (1, 2, 3):
                o2(d, False).wait_recv()
            own_out(o3, 0)
            own_out(o3, 1)

        @pl.when(c == 0)
        def _():
            rest_in(vx, n)
            for d in (1, 2, 3):
                vy(n, d, False).wait_recv()

        pair = lax.rem(y + s, 4)
        rhs = jnp.concatenate([gvb[q, pair].reshape(2048, 128) for q in range(2)], axis=1)
        lhs = t2[pl.ds(c * 2, 2)].reshape(512, 2048)
        h = jnp.dot(lhs, rhs, preferred_element_type=F32).astype(BF)
        for q in range(2):
            hs[c, pair * 2 + q] = h[:, q * 128:(q + 1) * 128].reshape(2, 256, 128)
        h_copy(c, s, 1, True).start()

        @pl.when(s == 0)
        def _():
            h_own(c).start()

        @pl.when(s > 0)
        def _():
            h_copy(c, s, 0, True).start()

        return carry

    lax.fori_loop(0, NC * 4, first, 0)

    for t in (0, 1):
        pass_on(o3, t)
        own_out(o3, t + 2)
    for t in (0, 1):
        rest_in(o3, t)
        o4(t, True).start()
        pass_on(o3, t + 2)

    def s_copy(c, d, e, mine):
        to = moved(p, x=d)
        frm = p if mine else moved(p, x=-d)
        if e:
            to = flip(to, "z")
            if not mine:
                frm = flip(frm, "z")
        frm_row = lax.rem(frm["z"], 2) * 4 + frm["x"]
        return remote(ss.at[c, d, e], out.at[pl.ds(frm_row * 8 + c * 2, 2)], sss.at[c, d, e], srs.at[c, d, e], to)

    def s_own(c):
        return pltpu.make_async_copy(ss.at[c, 0, 0], out.at[pl.ds(row * 8 + c * 2, 2)], sl.at[c])

    def lined_up(c, q):
        rows = []
        for b in range(16):
            for j in range(4):
                n = (b // 2) * 8 + j * 2 + b % 2
                rows.append(hr[c, q, n // 8, (n % 8) * 32:(n % 8) * 32 + 32, :])
        return jnp.concatenate(rows, axis=0)

    def second(j, carry):
        c, t = j // 4, lax.rem(j, 4)

        @pl.when(t == 0)
        def _():
            h_own(c).wait()
            h_copy(c, 0, 1, False).wait_recv()
            for s in (1, 2, 3):
                for e in (0, 1):
                    h_copy(c, s, e, False).wait_recv()

        @pl.when(c == 0)
        def _():
            @pl.when(t >= 2)
            def _():
                rest_in(o3, t)
                o4(t, True).start()

            o4(t, False).wait_recv()

        rows = pl.ds(pl.multiple_of(t * 256, 256), 256)
        lhs = jnp.concatenate(
            [
                jnp.concatenate(
                    [got[b // 8, (b // 2) % 4, b % 2, zl if e == 0 else 1 - zl, rows, :] for b in range(16)], axis=1
                )
                for e in (0, 1)
            ],
            axis=0,
        )
        rhs = jnp.concatenate([lined_up(c, q) for q in range(2)], axis=1)
        r = jnp.dot(lhs, rhs, preferred_element_type=F32).astype(BF)
        d = lax.rem(t - x + 4, 4)
        for e in (0, 1):
            for q in range(2):
                ss[c, d, e, q] = r[e * 256:(e + 1) * 256, q * 128:(q + 1) * 128]
        s_copy(c, d, 1, True).start()

        @pl.when(d == 0)
        def _():
            s_own(c).start()

        @pl.when(d > 0)
        def _():
            s_copy(c, d, 0, True).start()

        return carry

    lax.fori_loop(0, NC * 4, second, 0)

    v1_sibling(True).wait_send()
    for part in (0, 1):
        for d in (1, 2, 3):
            for e in (0, 1):
                v1(part, d, e, True).wait_send()
            v2(part, d, True).wait_send()
    for de in group:
        o1(*de, True).wait_send()
    for d in (1, 2, 3):
        o2(d, True).wait_send()

    def drain(c, carry):
        t_share(c, True).wait_send()
        for d in (1, 2, 3):
            vy(c, d, True).wait_send()
        for side in (0, 1):
            for n in range(3):
                vx(c, side, n, True).wait_send()
                o3(c, side, n, True).wait_send()
        o4(c, True).wait_send()
        s_own(c).wait()
        for s in range(4):
            for e in (0, 1):
                if s or e:
                    h_copy(c, s, e, True).wait_send()
                    s_copy(c, s, e, True).wait_send()
                    s_copy(c, s, e, False).wait_recv()
        return carry

    lax.fori_loop(0, NC, drain, 0)


def per_device(three_centre, green_virt, green_occ, pattern, block_sizes, atom_order):
    vmem = pl.BlockSpec(memory_space=pltpu.VMEM)
    dma = pltpu.SemaphoreType.DMA
    blocks = pl.pallas_call(
        kernel,
        out_shape=jax.ShapeDtypeStruct((64, 256, 128), BF),
        in_specs=[vmem, vmem, pl.BlockSpec(memory_space=pltpu.SMEM), vmem, vmem, pl.BlockSpec(memory_space=pl.ANY)],
        out_specs=pl.BlockSpec(memory_space=pl.ANY),
        scratch_shapes=[
            pltpu.VMEM((4, 16, 16, 128), F32),
            pltpu.VMEM((2, 2, 4, 16, 128), BF),
            pltpu.VMEM((2, 4, 2, 4, 4, 2, 32, 128), BF),
            pltpu.VMEM((8, 2, 128, 2048), BF),
            pltpu.VMEM((128, 2048), BF),
            pltpu.VMEM((NC, 8, 2, 256, 128), BF),
            pltpu.VMEM((NC, 2, 8, 256, 128), BF),
            pltpu.VMEM((8, 16, 1024), BF),
            pltpu.VMEM((2, 4, 2, 2, 1024, 128), BF),
            pltpu.VMEM((NC, 4, 2, 2, 256, 128), BF),
            dma((NC,)), dma((2,)), dma((NC,)), dma((NC,)),
            dma((3, 3, 2)), dma((3, 3, 2)), dma((2, 3)), dma((2, 3)), dma((4, 3)), dma((4, 3)), dma((4, 2, 3)), dma((4, 2, 3)),
            dma((4, 2)), dma((4, 2)), dma((3,)), dma((3,)), dma((4, 2, 3)), dma((4, 2, 3)), dma((4,)), dma((4,)),
            dma((NC, 4, 2)), dma((NC, 4, 2)), dma((NC,)), dma((NC, 4, 2)), dma((NC, 4, 2)), dma((NC,)),
        ],
        compiler_params=pltpu.CompilerParams(
            collective_id=0, has_side_effects=True, vmem_limit_bytes=56 * 2**20
        ),
        name="contract",
    )(green_virt, green_occ, atom_order, block_sizes.reshape(1, -1), pattern, three_centre)
    return jnp.transpose(blocks, (1, 0, 2))


def solution(mesh):
    in_specs = (P("row", "col", None), P(("row", "col"), None), P(("row", "col"), None), P(), P(), P())
    return jax.shard_map(
        per_device, mesh=mesh, in_specs=in_specs, out_specs=P("row", None, "col"), check_vma=False
    )
```

time: 158 us -> 143 us (0.905)
  the two profiles are of different devices: /device:TPU:21 before, /device:TPU:0 now
where the time goes in v2:
time: 143 us; the launch traced here: 141 us
  Pallas kernels  134 us (94%)
  local copies, waits for them, and re-layouts  6.9 us (5%)
    pallas_call x1, Pallas kernels, per_device(): pl.pallas_call(kernel, out_shape=jax.ShapeDtypeStruct((64, 256, 128), BF)...  134 us
    transpose x1, local copies, waits for them, and re-layouts, per_device(): return jnp.transpose(blocks, (1, 0, 2))  6.9 us

profile of v2, /device:TPU:0, one launch (start us, length us, event | category | flops | bytes accessed | tf_op | source)
XLA Modules:
  0.0 140.5 jit_solution(15138980777538151144)
XLA Ops:
  0.0 133.6 %contract.1 = bf16[64,256,128]{2,1,0:T(8,128)(2,1)} custom-call(bf16[16,2048]{1,0:T(8,128)(2,1)} %gv.1, bf16[16,2048]{1,0:T(8,128)(2,1)} %go.1, s32[64]{0:T(128)} %order.1, s32[1,64]{1,0:T(1,128)} %bitcast.3, s32[64,64]{1,0:T(8,128)} %pattern.1, bf16[8,128,2048]{2,1,0:T(8,128)(2,1)} %t_hbm.1), custom_call_target="tpu_custom_call" | custom-call | tf_op jit(solution)/shard_map/contract/pallas_call | solution.py:440
  133.6 6.9 %copy.7 = bf16[256,64,128]{2,1,0:T(8,128)(2,1)} copy(bf16[256,64,128]{2,0,1:T(8,128)(2,1)} %bitcast.2) | data formatting | bytes 8388608 | tf_op jit(solution)/shard_map/transpose | solution.py:466

commit v3 on v2

--- a/solution.py
+++ b/solution.py
@@ -9,7 +9,8 @@
 BF = jnp.bfloat16
 F32 = jnp.float32
 NC = 4
-ORDERS = ("yzx", "zxy")
+ORDERS = ("zyx", "zxy")
+FAR_ORDER = (1, 3, 2, 0)
 
 
 def me():
@@ -51,15 +52,14 @@
             found.append(moved(p, y=d, k=e))
             found.append(moved(p, z=d, k=e))
         found.append(moved(p, x=d))
-        found.append(moved(p, y=d, z=2))
         found.append(flip(moved(p, x=d), "z"))
     return found
 
 
 def kernel(gv, go, order, sizes, pattern, t_hbm, out,
-           turned, gp, gvb, t2, mask, hs, hr, gst, got, ss,
+           turned, gp, gvb, t2, mask, hs, hz, hr, gst, got, ss,
            t_sem, own_sem, ts_sem, tr_sem, v1s, v1r, v2s, v2r, vys, vyr, vxs, vxr,
-           o1s, o1r, o2s, o2r, o3s, o3r, o4s, o4r, hss, hrs, hl, sss, srs, sl):
+           o1s, o1r, o2s, o2r, o3s, o3r, o4s, o4r, hus, hur, hss, hrs, hl, sss, srs, sl):
     p = me()
     x, y, z, k = p["x"], p["y"], p["z"], p["k"]
     zl, zh, yl, yh = lax.rem(z, 2), z // 2, lax.rem(y, 2), y // 2
@@ -114,24 +114,22 @@
 
     pl.semaphore_wait(barrier, len(peers))
 
-    def v1(part, d, e, mine):
-        axis = ORDERS[part][0]
-        to = moved(p, **{axis: d, "k": e})
-        frm = p if mine else moved(p, **{axis: -d, "k": e})
-        dst = gvb.at[part, :, lax.rem(frm["z"], 2), frm["x"], frm["y"], frm["z"] // 2, rows16(frm["k"])]
-        return remote(gp.at[to["k"], part], dst, v1s.at[part, d - 1, e], v1r.at[part, d - 1, e], to)
+    def v1(d, e, mine):
+        to = moved(p, z=d, k=e)
+        frm = p if mine else moved(p, z=-d, k=e)
+        dst = gvb.at[:, :, lax.rem(frm["z"], 2), x, y, frm["z"] // 2, rows16(frm["k"])]
+        return remote(gp.at[to["k"]], dst, v1s.at[d - 1, e], v1r.at[d - 1, e], to)
 
     def v1_sibling(mine):
         frm = p if mine else moved(p, k=1)
         return remote(
-            gp.at[1 - k], gvb.at[:, :, zl, x, y, zh, rows16(frm["k"])], v1s.at[2, 0, 0], v1r.at[2, 0, 0], moved(p, k=1)
+            gp.at[1 - k], gvb.at[:, :, zl, x, y, zh, rows16(frm["k"])], v1s.at[3, 0], v1r.at[3, 0], moved(p, k=1)
         )
 
     v1_sibling(True).start()
     for d in (1, 3, 2):
-        for part in (0, 1):
-            for e in (0, 1):
-                v1(part, d, e, True).start()
+        for e in (0, 1):
+            v1(d, e, True).start()
 
     def o1(d, e, mine):
         to = moved(p, y=d, k=e)
@@ -178,21 +176,32 @@
 
     lax.fori_loop(0, NC, filter_chunk, 0)
 
-    def v2(part, d, mine):
+    def v2(part, j, d, mine):
         axis = ORDERS[part][1]
         at = p if mine else moved(p, **{axis: -d})
-        azl, azh = lax.rem(at["z"], 2), at["z"] // 2
-        slot = gvb.at[0, :, azl, x, :, azh] if part == 0 else gvb.at[1, :, :, at["x"], y, :]
-        return remote(slot, slot, v2s.at[part, d - 1], v2r.at[part, d - 1], moved(p, **{axis: d}))
+        if part == 0:
+            slot = gvb.at[0, lax.rem((y + d if mine else y) + turn(j), 4), :, x, at["y"], :]
+        else:
+            slot = gvb.at[1, lax.rem(y + FAR_ORDER[j], 4), :, at["x"], y, :]
+        return remote(slot, slot, v2s.at[part, j, d - 1], v2r.at[part, j, d - 1], moved(p, **{axis: d}))
+
+    def v2_out(part, j):
+        for d in (1, 3, 2):
+            v2(part, j, d, True).start()
+
+    def v2_in(part, j):
+        for d in (1, 2, 3):
+            v2(part, j, d, False).wait_recv()
 
     own.wait()
     v1_sibling(False).wait_recv()
-    for part in (0, 1):
-        for d in (1, 2, 3):
-            for e in (0, 1):
-                v1(part, d, e, False).wait_recv()
-        for d in (1, 3, 2):
-            v2(part, d, True).start()
+    for d in (1, 2, 3):
+        for e in (0, 1):
+            v1(d, e, False).wait_recv()
+    for j in range(4):
+        v2_out(0, j)
+        if j < 3:
+            v2_out(1, j)
 
     own_o.wait()
     for de in group:
@@ -245,51 +254,70 @@
         slot = got.at[:, :, :, k if mine else 1 - k, pl.ds(t * 256, 256)]
         return remote(slot, slot, o4s.at[t], o4r.at[t], moved(p, k=1))
 
-    for part in (0, 1):
-        for d in (1, 2, 3):
-            v2(part, d, False).wait_recv()
-
+    v2_in(0, 0)
     own_out(vx, 0)
-    own_out(vx, 1)
-
-    def vy_start(s, carry):
+    v2_out(1, 3)
+    for j in range(3):
+        v2_in(1, j)
+        vy(0, FAR_ORDER[j], True).start()
+    vy(1, 1, True).start()
+    vy(1, 2, True).start()
+    for j in range(1, 4):
+        v2_in(0, j)
+    v2_in(1, 3)
+    vy(1, 3, True).start()
+    for s in (2, 3):
         for d in (1, 3, 2):
             vy(s, d, True).start()
-        return carry
-
-    lax.fori_loop(0, 4, vy_start, 0)
 
     for c in range(NC):
         t_share(c, False).wait_recv()
-
-    def h_copy(c, s, e, mine):
-        to = moved(p, y=s, z=2 * e)
-        frm = p if mine else moved(p, y=-s, z=2 * e)
-        return remote(
-            hs.at[c, to["y"] * 2 + to["z"] // 2],
-            hr.at[c, :, frm["y"] * 2 + frm["z"] // 2],
-            hss.at[c, s, e], hrs.at[c, s, e], to,
-        )
 
     def h_own(c):
         chip = y * 2 + zh
         return pltpu.make_async_copy(hs.at[c, chip], hr.at[c, :, chip], hl.at[c])
 
+    def h_side(c, s, mine):
+        source = moved(p, y=0 if mine else -s)["y"] * 2 + zh
+        return remote(
+            hs.at[c, lax.rem(y + s, 4) * 2 + zh], hr.at[c, :, source], hss.at[c, s, 0], hrs.at[c, s, 0], moved(p, y=s)
+        )
+
+    def h_cross(c, s, mine):
+        if isinstance(s, int) and s == 0:
+            dst = hr.at[c, :, y * 2 + (zh if mine else 1 - zh)]
+        else:
+            dst = hz.at[c, s - 1]
+        return remote(
+            hs.at[c, lax.rem(y + s, 4) * 2 + 1 - zh], dst, hus.at[c, s], hur.at[c, s], moved(p, z=2)
+        )
+
+    def h_pass(c, s, mine):
+        source = moved(p, y=0 if mine else -s)["y"] * 2 + 1 - zh
+        return remote(hz.at[c, s - 1], hr.at[c, :, source], hss.at[c, s, 1], hrs.at[c, s, 1], moved(p, y=s))
+
+    def h_on(half, s):
+        for c in (half * 2, half * 2 + 1):
+            h_cross(c, s, False).wait_recv()
+            h_pass(c, s, True).start()
+
     def first(i, carry):
-        n, c = i // 4, lax.rem(i, 4)
+        half, n = i // 4, lax.rem(i, 4)
         s = turn(n)
 
         @pl.when(i == 0)
         def _():
-            for n in (0, 1):
-                pass_on(vx, n)
-                own_out(vx, n + 2)
-
-        @pl.when(i == 4)
-        def _():
+            pass_on(vx, 0)
+            own_out(vx, 1)
+            own_out(vx, 2)
+
+        @pl.when(i == 1)
+        def _():
+            pass_on(vx, 1)
+            own_out(vx, 3)
             pass_on(vx, 2)
 
-        @pl.when(i == 8)
+        @pl.when(i == 2)
         def _():
             pass_on(vx, 3)
             for d in (1, 2, 3):
@@ -297,39 +325,62 @@
             own_out(o3, 0)
             own_out(o3, 1)
 
-        @pl.when(c == 0)
+        @pl.when(half == 0)
         def _():
             rest_in(vx, n)
             for d in (1, 2, 3):
                 vy(n, d, False).wait_recv()
 
+        @pl.when(i == 4)
+        def _():
+            h_on(0, 1)
+            pass_on(o3, 0)
+            own_out(o3, 2)
+
+        @pl.when(i == 6)
+        def _():
+            h_on(0, 3)
+
         pair = lax.rem(y + s, 4)
         rhs = jnp.concatenate([gvb[q, pair].reshape(2048, 128) for q in range(2)], axis=1)
-        lhs = t2[pl.ds(c * 2, 2)].reshape(512, 2048)
+        lhs = t2[pl.ds(half * 4, 4)].reshape(1024, 2048)
         h = jnp.dot(lhs, rhs, preferred_element_type=F32).astype(BF)
-        for q in range(2):
-            hs[c, pair * 2 + q] = h[:, q * 128:(q + 1) * 128].reshape(2, 256, 128)
-        h_copy(c, s, 1, True).start()
-
-        @pl.when(s == 0)
-        def _():
-            h_own(c).start()
-
-        @pl.when(s > 0)
-        def _():
-            h_copy(c, s, 0, True).start()
+        for m in range(2):
+            for q in range(2):
+                hs[half * 2 + m, pair * 2 + q] = h[m * 512:(m + 1) * 512, q * 128:(q + 1) * 128].reshape(2, 256, 128)
+        for m in range(2):
+            c = half * 2 + m
+
+            @pl.when(n == 0)
+            def _():
+                h_cross(c, 0, True).start()
+                h_own(c).start()
+
+            @pl.when(n > 0)
+            def _():
+                h_cross(c, s, True).start()
+
+            @pl.when((n > 0) & (half == 0))
+            def _():
+                h_side(c, s, True).start()
 
         return carry
 
-    lax.fori_loop(0, NC * 4, first, 0)
-
-    for t in (0, 1):
-        pass_on(o3, t)
-        own_out(o3, t + 2)
-    for t in (0, 1):
-        rest_in(o3, t)
-        o4(t, True).start()
-        pass_on(o3, t + 2)
+    lax.fori_loop(0, 8, first, 0)
+
+    pass_on(o3, 1)
+    own_out(o3, 3)
+    h_on(0, 2)
+    for s in (1, 3, 2):
+        for c in (2, 3):
+            h_side(c, s, True).start()
+    rest_in(o3, 0)
+    o4(0, True).start()
+    pass_on(o3, 2)
+    rest_in(o3, 1)
+    o4(1, True).start()
+    h_on(1, 1)
+    pass_on(o3, 3)
 
     def s_copy(c, d, e, mine):
         to = moved(p, x=d)
@@ -353,22 +404,32 @@
         return jnp.concatenate(rows, axis=0)
 
     def second(j, carry):
-        c, t = j // 4, lax.rem(j, 4)
+        half, t = j // 4, lax.rem(j, 4)
 
         @pl.when(t == 0)
         def _():
-            h_own(c).wait()
-            h_copy(c, 0, 1, False).wait_recv()
-            for s in (1, 2, 3):
-                for e in (0, 1):
-                    h_copy(c, s, e, False).wait_recv()
-
-        @pl.when(c == 0)
+            for m in range(2):
+                c = half * 2 + m
+                h_own(c).wait()
+                h_cross(c, 0, False).wait_recv()
+                for s in (1, 2, 3):
+                    h_side(c, s, False).wait_recv()
+                    h_pass(c, s, False).wait_recv()
+
+        @pl.when(j == 2)
+        def _():
+            h_on(1, 3)
+
+        @pl.when(half == 0)
         def _():
             @pl.when(t >= 2)
             def _():
                 rest_in(o3, t)
                 o4(t, True).start()
+
+            @pl.when(t == 3)
+            def _():
+                h_on(1, 2)
 
             o4(t, False).wait_recv()
 
@@ -382,32 +443,44 @@
             ],
             axis=0,
         )
-        rhs = jnp.concatenate([lined_up(c, q) for q in range(2)], axis=1)
+        rhs = jnp.concatenate([lined_up(half * 2 + m, q) for m in range(2) for q in range(2)], axis=1)
         r = jnp.dot(lhs, rhs, preferred_element_type=F32).astype(BF)
         d = lax.rem(t - x + 4, 4)
+        for m in range(2):
+            c = half * 2 + m
+            for e in (0, 1):
+                for q in range(2):
+                    ss[c, d, e, q] = r[e * 256:(e + 1) * 256, (m * 2 + q) * 128:(m * 2 + q + 1) * 128]
+
+            @pl.when((d == 0) | (half == 1))
+            def _():
+                s_copy(c, d, 1, True).start()
+
+            @pl.when(d == 0)
+            def _():
+                s_own(c).start()
+
+            @pl.when(d > 0)
+            def _():
+                s_copy(c, d, 0, True).start()
+
+        @pl.when(j == 3)
+        def _():
+            for d1 in (1, 3, 2):
+                for c in (0, 1):
+                    s_copy(c, d1, 1, True).start()
+
+        return carry
+
+    lax.fori_loop(0, 8, second, 0)
+
+    v1_sibling(True).wait_send()
+    for d in (1, 2, 3):
         for e in (0, 1):
-            for q in range(2):
-                ss[c, d, e, q] = r[e * 256:(e + 1) * 256, q * 128:(q + 1) * 128]
-        s_copy(c, d, 1, True).start()
-
-        @pl.when(d == 0)
-        def _():
-            s_own(c).start()
-
-        @pl.when(d > 0)
-        def _():
-            s_copy(c, d, 0, True).start()
-
-        return carry
-
-    lax.fori_loop(0, NC * 4, second, 0)
-
-    v1_sibling(True).wait_send()
-    for part in (0, 1):
-        for d in (1, 2, 3):
-            for e in (0, 1):
-                v1(part, d, e, True).wait_send()
-            v2(part, d, True).wait_send()
+            v1(d, e, True).wait_send()
+        for part in (0, 1):
+            for j in range(4):
+                v2(part, j, d, True).wait_send()
     for de in group:
         o1(*de, True).wait_send()
     for d in (1, 2, 3):
@@ -423,15 +496,55 @@
                 o3(c, side, n, True).wait_send()
         o4(c, True).wait_send()
         s_own(c).wait()
+        h_cross(c, 0, True).wait_send()
+        for s in (1, 2, 3):
+            h_cross(c, s, True).wait_send()
+            h_side(c, s, True).wait_send()
+            h_pass(c, s, True).wait_send()
         for s in range(4):
             for e in (0, 1):
                 if s or e:
-                    h_copy(c, s, e, True).wait_send()
                     s_copy(c, s, e, True).wait_send()
                     s_copy(c, s, e, False).wait_recv()
         return carry
 
     lax.fori_loop(0, NC, drain, 0)
+
+
+def restack(blocks, out, source, target, in_sem, out_sem):
+    parts = in_sem.shape[0]
+    lams = out.shape[0] // parts
+
+    def load(i):
+        some = pl.ds(i * lams, lams)
+        return pltpu.make_async_copy(blocks.at[:, some], source.at[:, some], in_sem.at[i])
+
+    def store(i):
+        some = pl.ds(i * lams, lams)
+        return pltpu.make_async_copy(target.at[some], out.at[some], out_sem.at[i])
+
+    for i in range(parts):
+        load(i).start()
+    to = lax.broadcasted_iota(jnp.int32, (256, 256), 0)
+    frm = lax.broadcasted_iota(jnp.int32, (256, 256), 1)
+    one_hot = ((to // 16 == lax.rem(frm, 16)) & (lax.rem(to, 16) == frm // 16)).astype(BF)
+
+    def part(i, carry):
+        load(i).wait()
+        for pair in range(lams // 32):
+            for group in range(blocks.shape[0] // 16):
+                ps = slice(group * 16, group * 16 + 16)
+                at = [pl.ds(pl.multiple_of(i * lams + pair * 32 + h * 16, 16), 16) for h in range(2)]
+                rows = jnp.concatenate([source[ps, at[h], :].reshape(256, 128) for h in range(2)], axis=1)
+                moved_rows = jnp.dot(one_hot, rows, preferred_element_type=F32).astype(BF)
+                for h in range(2):
+                    target[at[h], ps, :] = moved_rows[:, h * 128:(h + 1) * 128].reshape(16, 16, 128)
+        store(i).start()
+        return carry
+
+    lax.fori_loop(0, parts, part, 0)
+    for i in range(parts):
+        store(i).wait()
 
 
 def per_device(three_centre, green_virt, green_occ, pattern, block_sizes, atom_order):
@@ -449,21 +562,31 @@
             pltpu.VMEM((8, 2, 128, 2048), BF),
             pltpu.VMEM((128, 2048), BF),
             pltpu.VMEM((NC, 8, 2, 256, 128), BF),
+            pltpu.VMEM((NC, 3, 2, 256, 128), BF),
             pltpu.VMEM((NC, 2, 8, 256, 128), BF),
             pltpu.VMEM((8, 16, 1024), BF),
             pltpu.VMEM((2, 4, 2, 2, 1024, 128), BF),
             pltpu.VMEM((NC, 4, 2, 2, 256, 128), BF),
             dma((NC,)), dma((2,)), dma((NC,)), dma((NC,)),
-            dma((3, 3, 2)), dma((3, 3, 2)), dma((2, 3)), dma((2, 3)), dma((4, 3)), dma((4, 3)), dma((4, 2, 3)), dma((4, 2, 3)),
+            dma((4, 2)), dma((4, 2)), dma((2, 4, 3)), dma((2, 4, 3)), dma((4, 3)), dma((4, 3)), dma((4, 2, 3)), dma((4, 2, 3)),
             dma((4, 2)), dma((4, 2)), dma((3,)), dma((3,)), dma((4, 2, 3)), dma((4, 2, 3)), dma((4,)), dma((4,)),
-            dma((NC, 4, 2)), dma((NC, 4, 2)), dma((NC,)), dma((NC, 4, 2)), dma((NC, 4, 2)), dma((NC,)),
+            dma((NC, 4)), dma((NC, 4)), dma((NC, 4, 2)), dma((NC, 4, 2)), dma((NC,)), dma((NC, 4, 2)), dma((NC, 4, 2)), dma((NC,)),
         ],
         compiler_params=pltpu.CompilerParams(
             collective_id=0, has_side_effects=True, vmem_limit_bytes=56 * 2**20
         ),
         name="contract",
     )(green_virt, green_occ, atom_order, block_sizes.reshape(1, -1), pattern, three_centre)
-    return jnp.transpose(blocks, (1, 0, 2))
+    anywhere = pl.BlockSpec(memory_space=pl.ANY)
+    return pl.pallas_call(
+        restack,
+        out_shape=jax.ShapeDtypeStruct((256, 64, 128), BF),
+        in_specs=[anywhere],
+        out_specs=anywhere,
+        scratch_shapes=[pltpu.VMEM((64, 256, 128), BF), pltpu.VMEM((256, 64, 128), BF), dma((2,)), dma((2,))],
+        compiler_params=pltpu.CompilerParams(vmem_limit_bytes=60 * 2**20),
+        name="restack",
+    )(blocks)
 
 
 def solution(mesh):

time: 143 us -> 138 us (0.965)
  local copies, waits for them, and re-layouts: 6.9 us -> 0 us
  Pallas kernels: 134 us -> 136 us
    transpose x1 -> x0, local copies, waits for them, and re-layouts: 6.9 us -> none  [per_device(): return jnp.transpose(blocks, (1, 0, 2))]
    pallas_call x0 -> x1, Pallas kernels: none -> 4.42 us  [per_device(): pl.pallas_call(restack, out_shape=jax.ShapeDtypeStruct((256, 64, 128), BF...]
    pallas_call x1, Pallas kernels: 134 us -> 132 us  [per_device(): pl.pallas_call(kernel, out_shape=jax.ShapeDtypeStruct((64, 256, 128), BF)...]
where the time goes in v3:
time: 138 us; the launch traced here: 136 us
  Pallas kernels  136 us (99%)
    pallas_call x1, Pallas kernels, per_device(): pl.pallas_call(kernel, out_shape=jax.ShapeDtypeStruct((64, 256, 128), BF)...  132 us
    pallas_call x1, Pallas kernels, per_device(): pl.pallas_call(restack, out_shape=jax.ShapeDtypeStruct((256, 64, 128), BF...  4.42 us

profile of v3, /device:TPU:0, one launch (start us, length us, event | category | flops | bytes accessed | tf_op | source)
XLA Modules:
  0.0 136.2 jit_solution(9595503521653406989)
XLA Ops:
  0.0 131.8 %contract.1.blocks = bf16[64,256,128]{2,1,0:T(8,128)(2,1)} custom-call(bf16[16,2048]{1,0:T(8,128)(2,1)} %gv.1, bf16[16,2048]{1,0:T(8,128)(2,1)} %go.1, s32[64]{0:T(128)} %order.1, s32[1,64]{1,0:T(1,128)} %bitcast.1, s32[64,64]{1,0:T(8,128)} %pattern.1, bf16[8,128,2048]{2,1,0:T(8,128)(2,1)} %t_hbm.1), custom_call_target="tpu_custom_call" | custom-call | tf_op jit(solution)/shard_map/contract/pallas_call | solution.py:553
  131.8 4.4 %restack.1 = bf16[256,64,128]{2,1,0:T(8,128)(2,1)} custom-call(bf16[64,256,128]{2,1,0:T(8,128)(2,1)} %contract.1.blocks), custom_call_target="tpu_custom_call" | custom-call | tf_op jit(solution)/shard_map/restack/pallas_call | solution.py:581

commit v4 on v3

--- a/solution.py
+++ b/solution.py
@@ -10,6 +10,7 @@
 F32 = jnp.float32
 NC = 4
 ORDERS = ("zyx", "zxy")
+TS, V1, V2, VY, VX, O1, O2, O3, O4, HC, HD, HP, SC, SD, SP = range(15)
 FAR_ORDER = (1, 3, 2, 0)
 
 
@@ -52,14 +53,12 @@
             found.append(moved(p, y=d, k=e))
             found.append(moved(p, z=d, k=e))
         found.append(moved(p, x=d))
-        found.append(flip(moved(p, x=d), "z"))
     return found
 
 
 def kernel(gv, go, order, sizes, pattern, t_hbm, out,
-           turned, gp, gvb, t2, mask, hs, hz, hr, gst, got, ss,
-           t_sem, own_sem, ts_sem, tr_sem, v1s, v1r, v2s, v2r, vys, vyr, vxs, vxr,
-           o1s, o1r, o2s, o2r, o3s, o3r, o4s, o4r, hus, hur, hss, hrs, hl, sss, srs, sl):
+           turned, gp, gvb, t2, mask, hs, hz, hr, gst, got, ss, sz,
+           t_sem, own_sem, sent, tr, v1r, v2r, vyr, vxr, o1r, o2r, o3r, o4r, hur, hrr, zr, srr):
     p = me()
     x, y, z, k = p["x"], p["y"], p["z"], p["k"]
     zl, zh, yl, yh = lax.rem(z, 2), z // 2, lax.rem(y, 2), y // 2
@@ -69,6 +68,9 @@
         return pltpu.make_async_remote_copy(
             src_ref=src, dst_ref=dst, send_sem=send, recv_sem=recv, device_id=device(to), device_id_type=MESH
         )
+
+    def arrived(ref, sem):
+        pltpu.make_async_copy(ref, ref, sem).wait()
 
     def t_load(c):
         two = pl.ds(c * 2, 2)
@@ -118,12 +120,12 @@
         to = moved(p, z=d, k=e)
         frm = p if mine else moved(p, z=-d, k=e)
         dst = gvb.at[:, :, lax.rem(frm["z"], 2), x, y, frm["z"] // 2, rows16(frm["k"])]
-        return remote(gp.at[to["k"]], dst, v1s.at[d - 1, e], v1r.at[d - 1, e], to)
+        return remote(gp.at[to["k"]], dst, sent.at[V1], v1r.at[0], to)
 
     def v1_sibling(mine):
         frm = p if mine else moved(p, k=1)
         return remote(
-            gp.at[1 - k], gvb.at[:, :, zl, x, y, zh, rows16(frm["k"])], v1s.at[3, 0], v1r.at[3, 0], moved(p, k=1)
+            gp.at[1 - k], gvb.at[:, :, zl, x, y, zh, rows16(frm["k"])], sent.at[V1], v1r.at[0], moved(p, k=1)
         )
 
     v1_sibling(True).start()
@@ -135,7 +137,7 @@
         to = moved(p, y=d, k=e)
         frm = p if mine else moved(p, y=-d, k=e)
         half = pl.ds(pl.multiple_of(to["k"] * 1024, 1024), 1024)
-        return remote(go.at[:, half], gst.at[frm["y"] * 2 + frm["k"]], o1s.at[d, e], o1r.at[d, e], to)
+        return remote(go.at[:, half], gst.at[frm["y"] * 2 + frm["k"]], sent.at[O1], o1r.at[0], to)
 
     group = [(d, e) for d in range(4) for e in (0, 1) if d or e]
     for de in group:
@@ -158,7 +160,7 @@
 
     def t_share(c, mine):
         part = t2.at[pl.ds(c * 2, 2), k if mine else 1 - k]
-        return remote(part, part, ts_sem.at[c], tr_sem.at[c], moved(p, k=1))
+        return remote(part, part, sent.at[TS], tr.at[0], moved(p, k=1))
 
     def filter_chunk(c, carry):
         t_load(c).wait()
@@ -183,35 +185,30 @@
             slot = gvb.at[0, lax.rem((y + d if mine else y) + turn(j), 4), :, x, at["y"], :]
         else:
             slot = gvb.at[1, lax.rem(y + FAR_ORDER[j], 4), :, at["x"], y, :]
-        return remote(slot, slot, v2s.at[part, j, d - 1], v2r.at[part, j, d - 1], moved(p, **{axis: d}))
+        return remote(slot, slot, sent.at[V2], v2r.at[part, j], moved(p, **{axis: d}))
 
     def v2_out(part, j):
         for d in (1, 3, 2):
             v2(part, j, d, True).start()
 
     def v2_in(part, j):
-        for d in (1, 2, 3):
-            v2(part, j, d, False).wait_recv()
+        arrived(got.at[0, 0, 0, 0, pl.ds(0, 384)], v2r.at[part, j])
 
     own.wait()
-    v1_sibling(False).wait_recv()
-    for d in (1, 2, 3):
-        for e in (0, 1):
-            v1(d, e, False).wait_recv()
+    arrived(got.at[0, 0, 0, 0, pl.ds(0, 896)], v1r.at[0])
     for j in range(4):
         v2_out(0, j)
         if j < 3:
             v2_out(1, j)
 
     own_o.wait()
-    for de in group:
-        o1(*de, False).wait_recv()
+    arrived(got.at[0, 0, 0, 0, pl.ds(0, 896)], o1r.at[0])
     got[zl, x, zh, k] = gst[...].reshape(128, 1024).T
 
     def o2(d, mine):
         at = p if mine else moved(p, z=-d)
         slot = got.at[lax.rem(at["z"], 2), x, at["z"] // 2, k]
-        return remote(slot, slot, o2s.at[d - 1], o2r.at[d - 1], moved(p, z=d))
+        return remote(slot, slot, sent.at[O2], o2r.at[0], moved(p, z=d))
 
     for d in (1, 3, 2):
         o2(d, True).start()
@@ -219,21 +216,21 @@
     def vy(s, d, mine):
         pair = lax.rem((y + d if mine else y) + turn(s), 4)
         slot = gvb.at[1, pair, :, :, y if mine else moved(p, y=-d)["y"], :]
-        return remote(slot, slot, vys.at[s, d - 1], vyr.at[s, d - 1], moved(p, y=d))
+        return remote(slot, slot, sent.at[VY], vyr.at[s], moved(p, y=d))
 
     def along_x(ref_of, send, recv, side, n, mine):
         step = 1 - 2 * side
         origin = (x if n < 2 else moved(p, x=-step)["x"]) if mine else moved(p, x=-step if n < 2 else 2)["x"]
         slot = ref_of(side if n == 2 else n, origin)
-        return remote(slot, slot, send.at[side, n], recv.at[side, n], moved(p, x=step))
+        return remote(slot, slot, send, recv.at[0 if n == side else 1], moved(p, x=step))
 
     def vx(s, side, n, mine):
         pair = lax.rem(y + turn(s), 4)
-        return along_x(lambda half, at: gvb.at[0, pair, half, at], vxs.at[s], vxr.at[s], side, n, mine)
+        return along_x(lambda half, at: gvb.at[0, pair, half, at], sent.at[VX], vxr.at[s], side, n, mine)
 
     def o3(t, side, n, mine):
         rows = pl.ds(t * 256, 256)
-        return along_x(lambda half, at: got.at[half, at, :, k, rows], o3s.at[t], o3r.at[t], side, n, mine)
+        return along_x(lambda half, at: got.at[half, at, :, k, rows], sent.at[O3], o3r.at[t], side, n, mine)
 
     def own_out(copy, i):
         for n in (0, 1):
@@ -241,18 +238,25 @@
                 copy(i, side, n if side == 0 else 1 - n, True).start()
 
     def pass_on(copy, i):
+        if copy is vx:
+            arrived(hs.at[0, 0], vxr.at[i, 0])
+        else:
+            arrived(hs.at[0, pl.ds(0, 2)], o3r.at[i, 0])
         for side in (0, 1):
-            copy(i, side, side, False).wait_recv()
             copy(i, side, 2, True).start()
 
     def rest_in(copy, i):
-        for side in (0, 1):
-            copy(i, side, 1 - side, False).wait_recv()
-            copy(i, side, 2, False).wait_recv()
+        if copy is vx:
+            arrived(hs.at[0, pl.ds(0, 2)], vxr.at[i, 1])
+        else:
+            arrived(hs.at[0, pl.ds(0, 4)], o3r.at[i, 1])
+
+    def vy_in(s):
+        arrived(hs.at[0, pl.ds(0, 3)], vyr.at[s])
 
     def o4(t, mine):
         slot = got.at[:, :, :, k if mine else 1 - k, pl.ds(t * 256, 256)]
-        return remote(slot, slot, o4s.at[t], o4r.at[t], moved(p, k=1))
+        return remote(slot, slot, sent.at[O4], o4r.at[t], moved(p, k=1))
 
     v2_in(0, 0)
     own_out(vx, 0)
@@ -270,31 +274,28 @@
         for d in (1, 3, 2):
             vy(s, d, True).start()
 
-    for c in range(NC):
-        t_share(c, False).wait_recv()
+    arrived(t2.at[:, 0], tr.at[0])
 
     def h_own(c):
         chip = y * 2 + zh
-        return pltpu.make_async_copy(hs.at[c, chip], hr.at[c, :, chip], hl.at[c])
+        return pltpu.make_async_copy(hs.at[c, chip], hr.at[c, :, chip], hrr.at[c // 2])
 
     def h_side(c, s, mine):
         source = moved(p, y=0 if mine else -s)["y"] * 2 + zh
         return remote(
-            hs.at[c, lax.rem(y + s, 4) * 2 + zh], hr.at[c, :, source], hss.at[c, s, 0], hrs.at[c, s, 0], moved(p, y=s)
+            hs.at[c, lax.rem(y + s, 4) * 2 + zh], hr.at[c, :, source], sent.at[HD], hrr.at[c // 2], moved(p, y=s)
         )
 
     def h_cross(c, s, mine):
         if isinstance(s, int) and s == 0:
-            dst = hr.at[c, :, y * 2 + (zh if mine else 1 - zh)]
+            dst, sem = hr.at[c, :, y * 2 + (zh if mine else 1 - zh)], hrr.at[c // 2]
         else:
-            dst = hz.at[c, s - 1]
-        return remote(
-            hs.at[c, lax.rem(y + s, 4) * 2 + 1 - zh], dst, hus.at[c, s], hur.at[c, s], moved(p, z=2)
-        )
+            dst, sem = hz.at[c, s - 1], hur.at[c, s]
+        return remote(hs.at[c, lax.rem(y + s, 4) * 2 + 1 - zh], dst, sent.at[HC], sem, moved(p, z=2))
 
     def h_pass(c, s, mine):
         source = moved(p, y=0 if mine else -s)["y"] * 2 + 1 - zh
-        return remote(hz.at[c, s - 1], hr.at[c, :, source], hss.at[c, s, 1], hrs.at[c, s, 1], moved(p, y=s))
+        return remote(hz.at[c, s - 1], hr.at[c, :, source], sent.at[HP], hrr.at[c // 2], moved(p, y=s))
 
     def h_on(half, s):
         for c in (half * 2, half * 2 + 1):
@@ -320,16 +321,14 @@
         @pl.when(i == 2)
         def _():
             pass_on(vx, 3)
-            for d in (1, 2, 3):
-                o2(d, False).wait_recv()
+            arrived(got.at[0, pl.ds(0, 3), 0, 0], o2r.at[0])
             own_out(o3, 0)
             own_out(o3, 1)
 
         @pl.when(half == 0)
         def _():
             rest_in(vx, n)
-            for d in (1, 2, 3):
-                vy(n, d, False).wait_recv()
+            vy_in(n)
 
         @pl.when(i == 4)
         def _():
@@ -382,18 +381,30 @@
     h_on(1, 1)
     pass_on(o3, 3)
 
-    def s_copy(c, d, e, mine):
-        to = moved(p, x=d)
-        frm = p if mine else moved(p, x=-d)
-        if e:
-            to = flip(to, "z")
-            if not mine:
-                frm = flip(frm, "z")
-        frm_row = lax.rem(frm["z"], 2) * 4 + frm["x"]
-        return remote(ss.at[c, d, e], out.at[pl.ds(frm_row * 8 + c * 2, 2)], sss.at[c, d, e], srs.at[c, d, e], to)
+    def s_slot(c, at):
+        return out.at[pl.ds((lax.rem(at["z"], 2) * 4 + at["x"]) * 8 + c * 2, 2)]
 
     def s_own(c):
-        return pltpu.make_async_copy(ss.at[c, 0, 0], out.at[pl.ds(row * 8 + c * 2, 2)], sl.at[c])
+        return pltpu.make_async_copy(ss.at[c, 0, 0], s_slot(c, p), srr.at[0])
+
+    def s_side(c, d):
+        return remote(ss.at[c, d, 0], s_slot(c, p), sent.at[SD], srr.at[0], moved(p, x=d))
+
+    def s_cross(c, d, straight):
+        dst, sem = (s_slot(c, p), srr.at[0]) if straight else (sz.at[c, d - 1], zr.at[c, d])
+        return remote(ss.at[c, d, 1], dst, sent.at[SC], sem, flip(p, "z"))
+
+    def s_on(half, d):
+        for c in (half * 2, half * 2 + 1):
+            s_cross(c, d, False).wait_recv()
+            remote(sz.at[c, d - 1], s_slot(c, flip(p, "z")), sent.at[SP], srr.at[0], moved(p, x=d)).start()
+
+    def s_on_tile(t):
+        d = lax.rem(t - x + 4, 4)
+
+        @pl.when(d > 0)
+        def _():
+            s_on(0, d)
 
     def lined_up(c, q):
         rows = []
@@ -404,17 +415,13 @@
         return jnp.concatenate(rows, axis=0)
 
     def second(j, carry):
-        half, t = j // 4, lax.rem(j, 4)
-
-        @pl.when(t == 0)
-        def _():
-            for m in range(2):
-                c = half * 2 + m
-                h_own(c).wait()
-                h_cross(c, 0, False).wait_recv()
-                for s in (1, 2, 3):
-                    h_side(c, s, False).wait_recv()
-                    h_pass(c, s, False).wait_recv()
+        half = j // 4
+        d = lax.rem(j + half + (1 - half) * (4 - x), 4)
+        t = lax.rem(x + d, 4)
+
+        @pl.when(lax.rem(j, 4) == 0)
+        def _():
+            arrived(hr.at[pl.ds(half * 2, 2)], hrr.at[half])
 
         @pl.when(j == 2)
         def _():
@@ -422,16 +429,16 @@
 
         @pl.when(half == 0)
         def _():
-            @pl.when(t >= 2)
-            def _():
-                rest_in(o3, t)
-                o4(t, True).start()
-
-            @pl.when(t == 3)
+            @pl.when(j >= 2)
+            def _():
+                rest_in(o3, j)
+                o4(j, True).start()
+
+            @pl.when(j == 3)
             def _():
                 h_on(1, 2)
 
-            o4(t, False).wait_recv()
+            o4(j, False).wait_recv()
 
         rows = pl.ds(pl.multiple_of(t * 256, 256), 256)
         lhs = jnp.concatenate(
@@ -445,70 +452,49 @@
         )
         rhs = jnp.concatenate([lined_up(half * 2 + m, q) for m in range(2) for q in range(2)], axis=1)
         r = jnp.dot(lhs, rhs, preferred_element_type=F32).astype(BF)
-        d = lax.rem(t - x + 4, 4)
         for m in range(2):
             c = half * 2 + m
             for e in (0, 1):
                 for q in range(2):
                     ss[c, d, e, q] = r[e * 256:(e + 1) * 256, (m * 2 + q) * 128:(m * 2 + q + 1) * 128]
 
-            @pl.when((d == 0) | (half == 1))
-            def _():
-                s_copy(c, d, 1, True).start()
-
             @pl.when(d == 0)
             def _():
+                s_cross(c, 0, True).start()
                 s_own(c).start()
 
             @pl.when(d > 0)
             def _():
-                s_copy(c, d, 0, True).start()
+                s_cross(c, d, False).start()
+                s_side(c, d).start()
 
         @pl.when(j == 3)
         def _():
-            for d1 in (1, 3, 2):
-                for c in (0, 1):
-                    s_copy(c, d1, 1, True).start()
+            s_on_tile(0)
+
+        @pl.when(j == 4)
+        def _():
+            s_on_tile(1)
 
         return carry
 
     lax.fori_loop(0, 8, second, 0)
-
-    v1_sibling(True).wait_send()
+    s_on_tile(2)
+    s_on_tile(3)
     for d in (1, 2, 3):
-        for e in (0, 1):
-            v1(d, e, True).wait_send()
-        for part in (0, 1):
-            for j in range(4):
-                v2(part, j, d, True).wait_send()
-    for de in group:
-        o1(*de, True).wait_send()
-    for d in (1, 2, 3):
-        o2(d, True).wait_send()
-
-    def drain(c, carry):
-        t_share(c, True).wait_send()
-        for d in (1, 2, 3):
-            vy(c, d, True).wait_send()
-        for side in (0, 1):
-            for n in range(3):
-                vx(c, side, n, True).wait_send()
-                o3(c, side, n, True).wait_send()
-        o4(c, True).wait_send()
-        s_own(c).wait()
-        h_cross(c, 0, True).wait_send()
-        for s in (1, 2, 3):
-            h_cross(c, s, True).wait_send()
-            h_side(c, s, True).wait_send()
-            h_pass(c, s, True).wait_send()
-        for s in range(4):
-            for e in (0, 1):
-                if s or e:
-                    s_copy(c, s, e, True).wait_send()
-                    s_copy(c, s, e, False).wait_recv()
-        return carry
-
-    lax.fori_loop(0, NC, drain, 0)
+        s_on(1, d)
+
+    arrived(out, srr.at[0])
+    arrived(t2.at[:, 0], sent.at[TS])
+    for kind, ref in (
+        (V1, got.at[0, 0, 0, 0, pl.ds(0, 896)]), (O1, got.at[0, 0, 0, 0, pl.ds(0, 896)]),
+        (V2, got.at[0, pl.ds(0, 3), 0, 0]), (O2, got.at[0, pl.ds(0, 3), 0, 0]),
+        (VY, got.at[0, pl.ds(0, 3), :, 0]), (VX, got.at[0, pl.ds(0, 3), :, 0]),
+        (O3, got.at[0, pl.ds(0, 3)]), (O4, got.at[0]),
+        (HC, got.at[0, pl.ds(0, 2)]), (HD, got.at[0, pl.ds(0, 3), :, 0]), (HP, got.at[0, pl.ds(0, 3), :, 0]),
+        (SC, got.at[0, pl.ds(0, 2)]), (SD, got.at[0, pl.ds(0, 3), :, 0]), (SP, got.at[0, pl.ds(0, 3), :, 0]),
+    ):
+        arrived(ref, sent.at[kind])
 
 
 def restack(blocks, out, source, target, in_sem, out_sem):
@@ -567,10 +553,9 @@
             pltpu.VMEM((8, 16, 1024), BF),
             pltpu.VMEM((2, 4, 2, 2, 1024, 128), BF),
             pltpu.VMEM((NC, 4, 2, 2, 256, 128), BF),
-            dma((NC,)), dma((2,)), dma((NC,)), dma((NC,)),
-            dma((4, 2)), dma((4, 2)), dma((2, 4, 3)), dma((2, 4, 3)), dma((4, 3)), dma((4, 3)), dma((4, 2, 3)), dma((4, 2, 3)),
-            dma((4, 2)), dma((4, 2)), dma((3,)), dma((3,)), dma((4, 2, 3)), dma((4, 2, 3)), dma((4,)), dma((4,)),
-            dma((NC, 4)), dma((NC, 4)), dma((NC, 4, 2)), dma((NC, 4, 2)), dma((NC,)), dma((NC, 4, 2)), dma((NC, 4, 2)), dma((NC,)),
+            pltpu.VMEM((NC, 3, 2, 256, 128), BF),
+            dma((NC,)), dma((2,)), dma((15,)), dma((1,)), dma((1,)), dma((2, 4)), dma((4,)), dma((4, 2)),
+            dma((1,)), dma((1,)), dma((4, 2)), dma((4,)), dma((NC, 4)), dma((2,)), dma((NC, 4)), dma((1,)),
         ],
         compiler_params=pltpu.CompilerParams(
             collective_id=0, has_side_effects=True, vmem_limit_bytes=56 * 2**20

time: 138 us -> 132 us (0.957)
  Pallas kernels: 136 us -> 131 us
    pallas_call x1, Pallas kernels: 132 us -> 126 us  [per_device(): pl.pallas_call(kernel, out_shape=jax.ShapeDtypeStruct((64, 256, 128), BF)...]
where the time goes in v4:
time: 132 us; the launch traced here: 131 us
  Pallas kernels  131 us (99%)
    pallas_call x1, Pallas kernels, per_device(): pl.pallas_call(kernel, out_shape=jax.ShapeDtypeStruct((64, 256, 128), BF)...  126 us
    pallas_call x1, Pallas kernels, per_device(): pl.pallas_call(restack, out_shape=jax.ShapeDtypeStruct((256, 64, 128), BF...  4.42 us

profile of v4, /device:TPU:0, one launch (start us, length us, event | category | flops | bytes accessed | tf_op | source)
XLA Modules:
  0.0 130.6 jit_solution(11558604868126237639)
XLA Ops:
  0.0 126.2 %contract.1.blocks = bf16[64,256,128]{2,1,0:T(8,128)(2,1)} custom-call(bf16[16,2048]{1,0:T(8,128)(2,1)} %gv.1, bf16[16,2048]{1,0:T(8,128)(2,1)} %go.1, s32[64]{0:T(128)} %order.1, s32[1,64]{1,0:T(1,128)} %bitcast.1, s32[64,64]{1,0:T(8,128)} %pattern.1, bf16[8,128,2048]{2,1,0:T(8,128)(2,1)} %t_hbm.1), custom_call_target="tpu_custom_call" | custom-call | tf_op jit(solution)/shard_map/contract/pallas_call | solution.py:539
  126.2 4.4 %restack.1 = bf16[256,64,128]{2,1,0:T(8,128)(2,1)} custom-call(bf16[64,256,128]{2,1,0:T(8,128)(2,1)} %contract.1.blocks), custom_call_target="tpu_custom_call" | custom-call | tf_op jit(solution)/shard_map/restack/pallas_call | solution.py:566

commit v5 on v4

--- a/solution.py
+++ b/solution.py
@@ -29,6 +29,14 @@
     return i + (i // 2) * (5 - 2 * i)
 
 
+def far_first(i):
+    return (2 + 3 * i + (i // 2) * (7 - 2 * i)) % 4 if isinstance(i, int) else lax.rem(2 + 3 * i + (i // 2) * (7 - 2 * i), 4)
+
+
+def stage(c):
+    return c // 2 + c // 3
+
+
 def device(p):
     return {"row": lax.rem(p["z"], 2) * 4 + p["x"], "col": (p["y"] * 2 + p["z"] // 2) * 2 + p["k"]}
 
@@ -56,8 +64,8 @@
     return found
 
 
-def kernel(gv, go, order, sizes, pattern, t_hbm, out,
-           turned, gp, gvb, t2, mask, hs, hz, hr, gst, got, ss, sz,
+def kernel(gv_hbm, go_hbm, order, sizes, pattern, t_hbm, out,
+           gv, go, turned, gp, gvb, t2, mask, hs, hz, hr, gst, got, ss, sz,
            t_sem, own_sem, sent, tr, v1r, v2r, vyr, vxr, o1r, o2r, o3r, o4r, hur, hrr, zr, srr):
     p = me()
     x, y, z, k = p["x"], p["y"], p["z"], p["k"]
@@ -76,15 +84,20 @@
         two = pl.ds(c * 2, 2)
         return pltpu.make_async_copy(t_hbm.at[two], t2.at[two, k], t_sem.at[c])
 
-    for c in range(NC):
-        t_load(c).start()
-
     barrier = pltpu.get_barrier_semaphore()
     peers = partners(p)
     for q in peers:
         pl.semaphore_signal(barrier, inc=1, device_id=device(q), device_id_type=MESH)
 
+    gv_load = pltpu.make_async_copy(gv_hbm, gv, own_sem.at[2])
+    go_load = pltpu.make_async_copy(go_hbm, go, own_sem.at[3])
+    gv_load.start()
+    go_load.start()
+    for c in range(NC):
+        t_load(c).start()
+
     lane_slot = lax.broadcasted_iota(jnp.int32, (16, 128), 1) // 32
+    gv_load.wait()
     for b in range(16):
         source = gv[:, b * 128:(b + 1) * 128].astype(F32)
         for t in range(4):
@@ -112,26 +125,21 @@
     own_o = pltpu.make_async_copy(
         go.at[:, pl.ds(pl.multiple_of(k * 1024, 1024), 1024)], gst.at[y * 2 + k], own_sem.at[1]
     )
+    go_load.wait()
     own_o.start()
 
     pl.semaphore_wait(barrier, len(peers))
 
-    def v1(d, e, mine):
+    def v1(part, d, e):
         to = moved(p, z=d, k=e)
-        frm = p if mine else moved(p, z=-d, k=e)
-        dst = gvb.at[:, :, lax.rem(frm["z"], 2), x, y, frm["z"] // 2, rows16(frm["k"])]
-        return remote(gp.at[to["k"]], dst, sent.at[V1], v1r.at[0], to)
-
-    def v1_sibling(mine):
-        frm = p if mine else moved(p, k=1)
         return remote(
-            gp.at[1 - k], gvb.at[:, :, zl, x, y, zh, rows16(frm["k"])], sent.at[V1], v1r.at[0], moved(p, k=1)
+            gp.at[to["k"], part], gvb.at[part, :, zl, x, y, zh, rows16(k)], sent.at[V1], v1r.at[part], to
         )
 
-    v1_sibling(True).start()
-    for d in (1, 3, 2):
-        for e in (0, 1):
-            v1(d, e, True).start()
+    v1_targets = [(0, 1)] + [(d, e) for d in (1, 3, 2) for e in (0, 1)]
+    for part in (1, 0):
+        for d, e in v1_targets:
+            v1(part, d, e).start()
 
     def o1(d, e, mine):
         to = moved(p, y=d, k=e)
@@ -192,18 +200,17 @@
             v2(part, j, d, True).start()
 
     def v2_in(part, j):
-        arrived(got.at[0, 0, 0, 0, pl.ds(0, 384)], v2r.at[part, j])
+        arrived(gst.at[pl.ds(0, 3)], v2r.at[part, j])
 
     own.wait()
-    arrived(got.at[0, 0, 0, 0, pl.ds(0, 896)], v1r.at[0])
-    for j in range(4):
-        v2_out(0, j)
-        if j < 3:
-            v2_out(1, j)
+    for part in (1, 0):
+        arrived(turned.at[0, pl.ds(0, 14)], v1r.at[part])
+        for j in range(3):
+            v2_out(part, j)
 
     own_o.wait()
-    arrived(got.at[0, 0, 0, 0, pl.ds(0, 896)], o1r.at[0])
-    got[zl, x, zh, k] = gst[...].reshape(128, 1024).T
+    arrived(gst.at[pl.ds(0, 7)], o1r.at[0])
+    got[zl, x, zh, k] = gst[...].reshape(128, 1024).T.reshape(4, 4, 64, 128)
 
     def o2(d, mine):
         at = p if mine else moved(p, z=-d)
@@ -229,8 +236,7 @@
         return along_x(lambda half, at: gvb.at[0, pair, half, at], sent.at[VX], vxr.at[s], side, n, mine)
 
     def o3(t, side, n, mine):
-        rows = pl.ds(t * 256, 256)
-        return along_x(lambda half, at: got.at[half, at, :, k, rows], sent.at[O3], o3r.at[t], side, n, mine)
+        return along_x(lambda half, at: got.at[half, at, :, k, :, t], sent.at[O3], o3r.at[t], side, n, mine)
 
     def own_out(copy, i):
         for n in (0, 1):
@@ -255,19 +261,25 @@
         arrived(hs.at[0, pl.ds(0, 3)], vyr.at[s])
 
     def o4(t, mine):
-        slot = got.at[:, :, :, k if mine else 1 - k, pl.ds(t * 256, 256)]
+        slot = got.at[:, :, :, k if mine else 1 - k, :, t]
         return remote(slot, slot, sent.at[O4], o4r.at[t], moved(p, k=1))
 
+    v2_in(1, 0)
+    vy(0, FAR_ORDER[0], True).start()
     v2_in(0, 0)
     own_out(vx, 0)
-    v2_out(1, 3)
-    for j in range(3):
+    for j in (1, 2):
         v2_in(1, j)
         vy(0, FAR_ORDER[j], True).start()
+    v2_out(1, 3)
+    v2_out(0, 3)
     vy(1, 1, True).start()
     vy(1, 2, True).start()
-    for j in range(1, 4):
-        v2_in(0, j)
+    v2_in(0, 1)
+    pass_on(vx, 0)
+    own_out(vx, 1)
+    v2_in(0, 2)
+    own_out(vx, 2)
     v2_in(1, 3)
     vy(1, 3, True).start()
     for s in (2, 3):
@@ -278,133 +290,148 @@
 
     def h_own(c):
         chip = y * 2 + zh
-        return pltpu.make_async_copy(hs.at[c, chip], hr.at[c, :, chip], hrr.at[c // 2])
+        return pltpu.make_async_copy(hs.at[c, chip], hr.at[c, :, chip], hrr.at[stage(c)])
 
     def h_side(c, s, mine):
         source = moved(p, y=0 if mine else -s)["y"] * 2 + zh
         return remote(
-            hs.at[c, lax.rem(y + s, 4) * 2 + zh], hr.at[c, :, source], sent.at[HD], hrr.at[c // 2], moved(p, y=s)
+            hs.at[c, lax.rem(y + s, 4) * 2 + zh], hr.at[c, :, source], sent.at[HD], hrr.at[stage(c)], moved(p, y=s)
         )
 
     def h_cross(c, s, mine):
         if isinstance(s, int) and s == 0:
-            dst, sem = hr.at[c, :, y * 2 + (zh if mine else 1 - zh)], hrr.at[c // 2]
+            dst, sem = hr.at[c, :, y * 2 + (zh if mine else 1 - zh)], hrr.at[stage(c)]
         else:
             dst, sem = hz.at[c, s - 1], hur.at[c, s]
         return remote(hs.at[c, lax.rem(y + s, 4) * 2 + 1 - zh], dst, sent.at[HC], sem, moved(p, z=2))
 
     def h_pass(c, s, mine):
         source = moved(p, y=0 if mine else -s)["y"] * 2 + 1 - zh
-        return remote(hz.at[c, s - 1], hr.at[c, :, source], sent.at[HP], hrr.at[c // 2], moved(p, y=s))
-
-    def h_on(half, s):
-        for c in (half * 2, half * 2 + 1):
-            h_cross(c, s, False).wait_recv()
-            h_pass(c, s, True).start()
-
-    def first(i, carry):
-        half, n = i // 4, lax.rem(i, 4)
+        return remote(hz.at[c, s - 1], hr.at[c, :, source], sent.at[HP], hrr.at[stage(c)], moved(p, y=s))
+
+    def h_on(c, s):
+        h_cross(c, s, False).wait_recv()
+        h_pass(c, s, True).start()
+
+    def first(half, n):
         s = turn(n)
-
-        @pl.when(i == 0)
-        def _():
-            pass_on(vx, 0)
-            own_out(vx, 1)
-            own_out(vx, 2)
-
-        @pl.when(i == 1)
+        pair = lax.rem(y + s, 4)
+        rhs = jnp.concatenate([gvb[q, pair].reshape(2048, 128) for q in range(2)], axis=1)
+        lhs = t2[pl.ds(half * 4, 4)].reshape(1024, 2048)
+        h = jnp.dot(lhs, rhs, preferred_element_type=F32).astype(BF)
+        for m in range(2):
+            c = half * 2 + m
+            for q in range(2):
+                hs[c, pair * 2 + q] = h[m * 512:(m + 1) * 512, q * 128:(q + 1) * 128].reshape(2, 256, 128)
+            if isinstance(n, int):
+                h_cross(c, s, True).start()
+                h_own(c).start()
+            elif half == 0:
+                h_cross(c, s, True).start()
+                h_side(c, s, True).start()
+            elif m == 0:
+                h_cross(c, s, True).start()
+
+    def first_own(half, carry):
+        first(half, 0)
+        return carry
+
+    def first_early(n, carry):
+        @pl.when(n == 1)
         def _():
             pass_on(vx, 1)
+            v2_in(0, 3)
             own_out(vx, 3)
             pass_on(vx, 2)
 
-        @pl.when(i == 2)
+        @pl.when(n == 2)
         def _():
             pass_on(vx, 3)
             arrived(got.at[0, pl.ds(0, 3), 0, 0], o2r.at[0])
             own_out(o3, 0)
             own_out(o3, 1)
 
-        @pl.when(half == 0)
-        def _():
-            rest_in(vx, n)
-            vy_in(n)
-
-        @pl.when(i == 4)
+        rest_in(vx, n)
+        vy_in(n)
+        first(0, n)
+        return carry
+
+    def first_late(n, carry):
+        @pl.when(n == 1)
         def _():
             h_on(0, 1)
+            h_on(1, 1)
             pass_on(o3, 0)
             own_out(o3, 2)
 
-        @pl.when(i == 6)
+        @pl.when(n == 3)
         def _():
             h_on(0, 3)
-
-        pair = lax.rem(y + s, 4)
-        rhs = jnp.concatenate([gvb[q, pair].reshape(2048, 128) for q in range(2)], axis=1)
-        lhs = t2[pl.ds(half * 4, 4)].reshape(1024, 2048)
-        h = jnp.dot(lhs, rhs, preferred_element_type=F32).astype(BF)
-        for m in range(2):
-            for q in range(2):
-                hs[half * 2 + m, pair * 2 + q] = h[m * 512:(m + 1) * 512, q * 128:(q + 1) * 128].reshape(2, 256, 128)
-        for m in range(2):
-            c = half * 2 + m
-
-            @pl.when(n == 0)
-            def _():
-                h_cross(c, 0, True).start()
-                h_own(c).start()
-
-            @pl.when(n > 0)
-            def _():
-                h_cross(c, s, True).start()
-
-            @pl.when((n > 0) & (half == 0))
-            def _():
-                h_side(c, s, True).start()
-
-        return carry
-
-    lax.fori_loop(0, 8, first, 0)
-
+            h_on(1, 3)
+
+        first(1, n)
+        return carry
+
+    rest_in(vx, 0)
+    vy_in(0)
+    lax.fori_loop(0, 2, first_own, 0)
+    lax.fori_loop(1, 4, first_early, 0)
+    lax.fori_loop(1, 4, first_late, 0)
+
+    for s in (1, 3, 2):
+        h_cross(3, s, True).start()
     pass_on(o3, 1)
     own_out(o3, 3)
     h_on(0, 2)
+    h_on(1, 2)
     for s in (1, 3, 2):
-        for c in (2, 3):
-            h_side(c, s, True).start()
+        h_side(2, s, True).start()
     rest_in(o3, 0)
     o4(0, True).start()
     pass_on(o3, 2)
+    h_on(2, 1)
     rest_in(o3, 1)
     o4(1, True).start()
-    h_on(1, 1)
+    h_on(2, 3)
     pass_on(o3, 3)
 
-    def s_slot(c, at):
-        return out.at[pl.ds((lax.rem(at["z"], 2) * 4 + at["x"]) * 8 + c * 2, 2)]
-
-    def s_own(c):
-        return pltpu.make_async_copy(ss.at[c, 0, 0], s_slot(c, p), srr.at[0])
-
-    def s_side(c, d):
-        return remote(ss.at[c, d, 0], s_slot(c, p), sent.at[SD], srr.at[0], moved(p, x=d))
-
-    def s_cross(c, d, straight):
-        dst, sem = (s_slot(c, p), srr.at[0]) if straight else (sz.at[c, d - 1], zr.at[c, d])
-        return remote(ss.at[c, d, 1], dst, sent.at[SC], sem, flip(p, "z"))
-
-    def s_on(half, d):
-        for c in (half * 2, half * 2 + 1):
-            s_cross(c, d, False).wait_recv()
-            remote(sz.at[c, d - 1], s_slot(c, flip(p, "z")), sent.at[SP], srr.at[0], moved(p, x=d)).start()
-
-    def s_on_tile(t):
-        d = lax.rem(t - x + 4, 4)
-
-        @pl.when(d > 0)
-        def _():
-            s_on(0, d)
+    whole = pl.ds(0, 256)
+
+    def s_slot(c, at, rows):
+        return out.at[pl.ds((lax.rem(at["z"], 2) * 4 + at["x"]) * 8 + c * 2, 2), rows]
+
+    def s_out(c, d, rows, part):
+        block = ss.at[c, lax.rem(x + d, 4)]
+
+        def stay():
+            pltpu.make_async_copy(block.at[0, :, rows], s_slot(c, p, rows), srr.at[0]).start()
+            remote(block.at[1, :, rows], s_slot(c, p, rows), sent.at[SC], srr.at[0], flip(p, "z")).start()
+
+        def leave():
+            s_cross(c, d, rows, part).start()
+            remote(block.at[0, :, rows], s_slot(c, p, rows), sent.at[SD], srr.at[0], moved(p, x=d)).start()
+
+        if isinstance(d, int):
+            leave() if d else stay()
+        else:
+            pl.when(d == 0)(stay)
+            pl.when(d > 0)(leave)
+
+    def s_cross(c, d, rows, part):
+        return remote(
+            ss.at[c, lax.rem(x + d, 4), 1, :, rows], sz.at[c, d - 1, :, rows], sent.at[SC], zr.at[part, c, d], flip(p, "z")
+        )
+
+    def s_on(c, d, rows, part):
+        s_cross(c, d, rows, part).wait_recv()
+        remote(
+            sz.at[c, d - 1, :, rows], s_slot(c, flip(p, "z"), rows), sent.at[SP], srr.at[0], moved(p, x=d)
+        ).start()
+
+    def s_on_early(part):
+        for i in range(3):
+            for c in (0, 1):
+                s_on(c, far_first(i), pl.ds(part * 128, 128), part)
 
     def lined_up(c, q):
         rows = []
@@ -414,80 +441,93 @@
                 rows.append(hr[c, q, n // 8, (n % 8) * 32:(n % 8) * 32 + 32, :])
         return jnp.concatenate(rows, axis=0)
 
-    def second(j, carry):
-        half = j // 4
-        d = lax.rem(j + half + (1 - half) * (4 - x), 4)
-        t = lax.rem(x + d, 4)
-
-        @pl.when(lax.rem(j, 4) == 0)
-        def _():
-            arrived(hr.at[pl.ds(half * 2, 2)], hrr.at[half])
-
-        @pl.when(j == 2)
-        def _():
-            h_on(1, 3)
-
-        @pl.when(half == 0)
-        def _():
-            @pl.when(j >= 2)
-            def _():
-                rest_in(o3, j)
-                o4(j, True).start()
-
-            @pl.when(j == 3)
-            def _():
-                h_on(1, 2)
-
-            o4(j, False).wait_recv()
-
-        rows = pl.ds(pl.multiple_of(t * 256, 256), 256)
+    def second(chunks, rows_of):
         lhs = jnp.concatenate(
             [
                 jnp.concatenate(
-                    [got[b // 8, (b // 2) % 4, b % 2, zl if e == 0 else 1 - zl, rows, :] for b in range(16)], axis=1
+                    [
+                        rows_of(got.at[b // 8, (b // 2) % 4, b % 2, zl if e == 0 else 1 - zl]).reshape(256, 128)
+                        for b in range(16)
+                    ],
+                    axis=1,
                 )
                 for e in (0, 1)
             ],
             axis=0,
         )
-        rhs = jnp.concatenate([lined_up(half * 2 + m, q) for m in range(2) for q in range(2)], axis=1)
-        r = jnp.dot(lhs, rhs, preferred_element_type=F32).astype(BF)
-        for m in range(2):
-            c = half * 2 + m
+        rhs = jnp.concatenate([lined_up(c, q) for c in chunks for q in range(2)], axis=1)
+        return jnp.dot(lhs, rhs, preferred_element_type=F32).astype(BF)
+
+    arrived(hr.at[pl.ds(0, 2)], hrr.at[0])
+
+    def second_early(t, carry):
+        @pl.when(t == 2)
+        def _():
+            h_on(2, 2)
+            for s in (1, 3, 2):
+                h_side(3, s, True).start()
+            h_on(3, 1)
+            rest_in(o3, 2)
+            o4(2, True).start()
+
+        @pl.when(t == 3)
+        def _():
+            rest_in(o3, 3)
+            o4(3, True).start()
+            h_on(3, 3)
+
+        o4(t, False).wait_recv()
+        r = second((0, 1), lambda ref: ref[:, t])
+        rows = pl.ds(pl.multiple_of(t * 64, 64), 64)
+        for c in (0, 1):
+            for owner in range(4):
+                for e in (0, 1):
+                    at = e * 256 + owner * 64
+                    for q in range(2):
+                        ss[c, owner, e, q, rows] = r[at:at + 64, (c * 2 + q) * 128:(c * 2 + q + 1) * 128]
+
+        for part in (0, 1):
+
+            @pl.when(t == part * 2 + 1)
+            def _():
+                for i in range(4):
+                    for c in (0, 1):
+                        s_out(c, far_first(i), pl.ds(part * 128, 128), part)
+
+        return carry
+
+    lax.fori_loop(0, 4, second_early, 0)
+    h_on(3, 2)
+
+    def second_late(c, carry):
+        arrived(hr.at[c], hrr.at[c - 1])
+
+        def tile(i, inner):
+            d = far_first(i)
+            owner = lax.rem(x + d, 4)
+            r = second((c,), lambda ref: ref[owner])
             for e in (0, 1):
                 for q in range(2):
-                    ss[c, d, e, q] = r[e * 256:(e + 1) * 256, (m * 2 + q) * 128:(m * 2 + q + 1) * 128]
-
-            @pl.when(d == 0)
-            def _():
-                s_cross(c, 0, True).start()
-                s_own(c).start()
-
-            @pl.when(d > 0)
-            def _():
-                s_cross(c, d, False).start()
-                s_side(c, d).start()
-
-        @pl.when(j == 3)
-        def _():
-            s_on_tile(0)
-
-        @pl.when(j == 4)
-        def _():
-            s_on_tile(1)
-
-        return carry
-
-    lax.fori_loop(0, 8, second, 0)
-    s_on_tile(2)
-    s_on_tile(3)
-    for d in (1, 2, 3):
-        s_on(1, d)
+                    ss[c, owner, e, q] = r[e * 256:(e + 1) * 256, q * 128:(q + 1) * 128]
+            s_out(c, d, whole, 0)
+            return inner
+
+        lax.fori_loop(0, 4, tile, 0)
+        s_on_early(c - 2)
+        return carry
+
+    lax.fori_loop(2, 4, second_late, 0)
+
+    def s_on_late(i, carry):
+        s_on(2 + i // 3, far_first(lax.rem(i, 3)), whole, 0)
+        return carry
+
+    lax.fori_loop(0, 6, s_on_late, 0)
 
     arrived(out, srr.at[0])
     arrived(t2.at[:, 0], sent.at[TS])
     for kind, ref in (
-        (V1, got.at[0, 0, 0, 0, pl.ds(0, 896)]), (O1, got.at[0, 0, 0, 0, pl.ds(0, 896)]),
+        (V1, gst.at[pl.ds(0, 7)]), (O1, gst.at[pl.ds(0, 7)]),
         (V2, got.at[0, pl.ds(0, 3), 0, 0]), (O2, got.at[0, pl.ds(0, 3), 0, 0]),
         (VY, got.at[0, pl.ds(0, 3), :, 0]), (VX, got.at[0, pl.ds(0, 3), :, 0]),
         (O3, got.at[0, pl.ds(0, 3)]), (O4, got.at[0]),
@@ -535,13 +575,16 @@
 
 def per_device(three_centre, green_virt, green_occ, pattern, block_sizes, atom_order):
     vmem = pl.BlockSpec(memory_space=pltpu.VMEM)
+    anywhere = pl.BlockSpec(memory_space=pl.ANY)
     dma = pltpu.SemaphoreType.DMA
     blocks = pl.pallas_call(
         kernel,
         out_shape=jax.ShapeDtypeStruct((64, 256, 128), BF),
-        in_specs=[vmem, vmem, pl.BlockSpec(memory_space=pltpu.SMEM), vmem, vmem, pl.BlockSpec(memory_space=pl.ANY)],
-        out_specs=pl.BlockSpec(memory_space=pl.ANY),
+        in_specs=[anywhere, anywhere, pl.BlockSpec(memory_space=pltpu.SMEM), vmem, vmem, anywhere],
+        out_specs=anywhere,
         scratch_shapes=[
+            pltpu.VMEM((16, 2048), BF),
+            pltpu.VMEM((16, 2048), BF),
             pltpu.VMEM((4, 16, 16, 128), F32),
             pltpu.VMEM((2, 2, 4, 16, 128), BF),
             pltpu.VMEM((2, 4, 2, 4, 4, 2, 32, 128), BF),
@@ -551,18 +594,17 @@
             pltpu.VMEM((NC, 3, 2, 256, 128), BF),
             pltpu.VMEM((NC, 2, 8, 256, 128), BF),
             pltpu.VMEM((8, 16, 1024), BF),
-            pltpu.VMEM((2, 4, 2, 2, 1024, 128), BF),
+            pltpu.VMEM((2, 4, 2, 2, 4, 4, 64, 128), BF),
             pltpu.VMEM((NC, 4, 2, 2, 256, 128), BF),
             pltpu.VMEM((NC, 3, 2, 256, 128), BF),
-            dma((NC,)), dma((2,)), dma((15,)), dma((1,)), dma((1,)), dma((2, 4)), dma((4,)), dma((4, 2)),
-            dma((1,)), dma((1,)), dma((4, 2)), dma((4,)), dma((NC, 4)), dma((2,)), dma((NC, 4)), dma((1,)),
+            dma((NC,)), dma((4,)), dma((15,)), dma((1,)), dma((2,)), dma((2, 4)), dma((4,)), dma((4, 2)),
+            dma((1,)), dma((1,)), dma((4, 2)), dma((4,)), dma((NC, 4)), dma((3,)), dma((2, NC, 4)), dma((1,)),
         ],
         compiler_params=pltpu.CompilerParams(
             collective_id=0, has_side_effects=True, vmem_limit_bytes=56 * 2**20
         ),
         name="contract",
     )(green_virt, green_occ, atom_order, block_sizes.reshape(1, -1), pattern, three_centre)
-    anywhere = pl.BlockSpec(memory_space=pl.ANY)
     return pl.pallas_call(
         restack,
         out_shape=jax.ShapeDtypeStruct((256, 64, 128), BF),

time: 132 us -> 126 us (0.955)
  Pallas kernels: 131 us -> 126 us
    pallas_call x1, Pallas kernels: 126 us -> 121 us  [per_device(): pl.pallas_call(kernel, out_shape=jax.ShapeDtypeStruct((64, 256, 128), BF)...]
where the time goes in v5:
time: 126 us
  Pallas kernels  126 us (100%)
    pallas_call x1, Pallas kernels, per_device(): pl.pallas_call(kernel, out_shape=jax.ShapeDtypeStruct((64, 256, 128), BF)...  121 us
    pallas_call x1, Pallas kernels, per_device(): pl.pallas_call(restack, out_shape=jax.ShapeDtypeStruct((256, 64, 128), BF...  4.41 us

profile of v5, /device:TPU:0, one launch (start us, length us, event | category | flops | bytes accessed | tf_op | source)
XLA Modules:
  0.0 125.6 jit_solution(6765598893508362118)
XLA Ops:
  0.0 121.2 %contract.1.blocks = bf16[64,256,128]{2,1,0:T(8,128)(2,1)} custom-call(bf16[16,2048]{1,0:T(8,128)(2,1)} %gv_hbm.1, bf16[16,2048]{1,0:T(8,128)(2,1)} %go_hbm.1, s32[64]{0:T(128)} %order.1, s32[1,64]{1,0:T(1,128)} %bitcast.1, s32[64,64]{1,0:T(8,128)} %pattern.1, bf16[8,128,2048]{2,1,0:T(8,128)(2,1)} %t_hbm.1), custom_call_target="tpu_custom_call" | custom-call | tf_op jit(solution)/shard_map/contract/pallas_call | solution.py:580
  121.2 4.4 %restack.1 = bf16[256,64,128]{2,1,0:T(8,128)(2,1)} custom-call(bf16[64,256,128]{2,1,0:T(8,128)(2,1)} %contract.1.blocks), custom_call_target="tpu_custom_call" | custom-call | tf_op jit(solution)/shard_map/restack/pallas_call | solution.py:608

commit v6 on v5

--- a/solution.py
+++ b/solution.py
@@ -64,8 +64,8 @@
     return found
 
 
-def kernel(gv_hbm, go_hbm, order, sizes, pattern, t_hbm, out,
-           gv, go, turned, gp, gvb, t2, mask, hs, hz, hr, gst, got, ss, sz,
+def kernel(gv, go, order, sizes, pattern, t_hbm, out,
+           turned, gp, gvb, t2, mask, hs, hz, hr, gst, got, ss, sz,
            t_sem, own_sem, sent, tr, v1r, v2r, vyr, vxr, o1r, o2r, o3r, o4r, hur, hrr, zr, srr):
     p = me()
     x, y, z, k = p["x"], p["y"], p["z"], p["k"]
@@ -89,15 +89,10 @@
     for q in peers:
         pl.semaphore_signal(barrier, inc=1, device_id=device(q), device_id_type=MESH)
 
-    gv_load = pltpu.make_async_copy(gv_hbm, gv, own_sem.at[2])
-    go_load = pltpu.make_async_copy(go_hbm, go, own_sem.at[3])
-    gv_load.start()
-    go_load.start()
     for c in range(NC):
         t_load(c).start()
 
     lane_slot = lax.broadcasted_iota(jnp.int32, (16, 128), 1) // 32
-    gv_load.wait()
     for b in range(16):
         source = gv[:, b * 128:(b + 1) * 128].astype(F32)
         for t in range(4):
@@ -125,7 +120,6 @@
     own_o = pltpu.make_async_copy(
         go.at[:, pl.ds(pl.multiple_of(k * 1024, 1024), 1024)], gst.at[y * 2 + k], own_sem.at[1]
     )
-    go_load.wait()
     own_o.start()
 
     pl.semaphore_wait(barrier, len(peers))
@@ -313,27 +307,19 @@
         h_cross(c, s, False).wait_recv()
         h_pass(c, s, True).start()
 
-    def first(half, n):
-        s = turn(n)
-        pair = lax.rem(y + s, 4)
+    def first(c0, chunks, n):
+        pair = lax.rem(y + turn(n), 4)
         rhs = jnp.concatenate([gvb[q, pair].reshape(2048, 128) for q in range(2)], axis=1)
-        lhs = t2[pl.ds(half * 4, 4)].reshape(1024, 2048)
+        lhs = t2[pl.ds(c0 * 2, chunks * 2)].reshape(chunks * 512, 2048)
         h = jnp.dot(lhs, rhs, preferred_element_type=F32).astype(BF)
-        for m in range(2):
-            c = half * 2 + m
+        for m in range(chunks):
             for q in range(2):
-                hs[c, pair * 2 + q] = h[m * 512:(m + 1) * 512, q * 128:(q + 1) * 128].reshape(2, 256, 128)
-            if isinstance(n, int):
-                h_cross(c, s, True).start()
-                h_own(c).start()
-            elif half == 0:
-                h_cross(c, s, True).start()
-                h_side(c, s, True).start()
-            elif m == 0:
-                h_cross(c, s, True).start()
-
-    def first_own(half, carry):
-        first(half, 0)
+                hs[c0 + m, pair * 2 + q] = h[m * 512:(m + 1) * 512, q * 128:(q + 1) * 128].reshape(2, 256, 128)
+
+    def first_own(c, carry):
+        first(c, 1, 0)
+        h_cross(c, 0, True).start()
+        h_own(c).start()
         return carry
 
     def first_early(n, carry):
@@ -353,7 +339,10 @@
 
         rest_in(vx, n)
         vy_in(n)
-        first(0, n)
+        first(0, 2, n)
+        for c in (0, 1):
+            h_cross(c, turn(n), True).start()
+            h_side(c, turn(n), True).start()
         return carry
 
     def first_late(n, carry):
@@ -369,12 +358,13 @@
             h_on(0, 3)
             h_on(1, 3)
 
-        first(1, n)
+        first(2, 2, n)
+        h_cross(2, turn(n), True).start()
         return carry
 
     rest_in(vx, 0)
     vy_in(0)
-    lax.fori_loop(0, 2, first_own, 0)
+    lax.fori_loop(0, NC, first_own, 0)
     lax.fori_loop(1, 4, first_early, 0)
     lax.fori_loop(1, 4, first_late, 0)
 
@@ -537,28 +527,21 @@
         arrived(ref, sent.at[kind])
 
 
-def restack(blocks, out, source, target, in_sem, out_sem):
-    parts = in_sem.shape[0]
+def restack(source, out, target, out_sem):
+    parts = out_sem.shape[0]
     lams = out.shape[0] // parts
-
-    def load(i):
-        some = pl.ds(i * lams, lams)
-        return pltpu.make_async_copy(blocks.at[:, some], source.at[:, some], in_sem.at[i])
 
     def store(i):
         some = pl.ds(i * lams, lams)
         return pltpu.make_async_copy(target.at[some], out.at[some], out_sem.at[i])
 
-    for i in range(parts):
-        load(i).start()
     to = lax.broadcasted_iota(jnp.int32, (256, 256), 0)
     frm = lax.broadcasted_iota(jnp.int32, (256, 256), 1)
     one_hot = ((to // 16 == lax.rem(frm, 16)) & (lax.rem(to, 16) == frm // 16)).astype(BF)
 
     def part(i, carry):
-        load(i).wait()
         for pair in range(lams // 32):
-            for group in range(blocks.shape[0] // 16):
+            for group in range(source.shape[0] // 16):
                 ps = slice(group * 16, group * 16 + 16)
                 at = [pl.ds(pl.multiple_of(i * lams + pair * 32 + h * 16, 16), 16) for h in range(2)]
                 rows = jnp.concatenate([source[ps, at[h], :].reshape(256, 128) for h in range(2)], axis=1)
@@ -579,12 +562,10 @@
     dma = pltpu.SemaphoreType.DMA
     blocks = pl.pallas_call(
         kernel,
-        out_shape=jax.ShapeDtypeStruct((64, 256, 128), BF),
-        in_specs=[anywhere, anywhere, pl.BlockSpec(memory_space=pltpu.SMEM), vmem, vmem, anywhere],
-        out_specs=anywhere,
+        out_shape=pltpu.VMEM((64, 256, 128), BF),
+        in_specs=[vmem, vmem, pl.BlockSpec(memory_space=pltpu.SMEM), vmem, vmem, anywhere],
+        out_specs=vmem,
         scratch_shapes=[
-            pltpu.VMEM((16, 2048), BF),
-            pltpu.VMEM((16, 2048), BF),
             pltpu.VMEM((4, 16, 16, 128), F32),
             pltpu.VMEM((2, 2, 4, 16, 128), BF),
             pltpu.VMEM((2, 4, 2, 4, 4, 2, 32, 128), BF),
@@ -597,7 +578,7 @@
             pltpu.VMEM((2, 4, 2, 2, 4, 4, 64, 128), BF),
             pltpu.VMEM((NC, 4, 2, 2, 256, 128), BF),
             pltpu.VMEM((NC, 3, 2, 256, 128), BF),
-            dma((NC,)), dma((4,)), dma((15,)), dma((1,)), dma((2,)), dma((2, 4)), dma((4,)), dma((4, 2)),
+            dma((NC,)), dma((2,)), dma((15,)), dma((1,)), dma((2,)), dma((2, 4)), dma((4,)), dma((4, 2)),
             dma((1,)), dma((1,)), dma((4, 2)), dma((4,)), dma((NC, 4)), dma((3,)), dma((2, NC, 4)), dma((1,)),
         ],
         compiler_params=pltpu.CompilerParams(
@@ -608,10 +589,10 @@
     return pl.pallas_call(
         restack,
         out_shape=jax.ShapeDtypeStruct((256, 64, 128), BF),
-        in_specs=[anywhere],
+        in_specs=[vmem],
         out_specs=anywhere,
-        scratch_shapes=[pltpu.VMEM((64, 256, 128), BF), pltpu.VMEM((256, 64, 128), BF), dma((2,)), dma((2,))],
-        compiler_params=pltpu.CompilerParams(vmem_limit_bytes=60 * 2**20),
+        scratch_shapes=[pltpu.VMEM((256, 64, 128), BF), dma((2,))],
+        compiler_params=pltpu.CompilerParams(vmem_limit_bytes=40 * 2**20),
         name="restack",
     )(blocks)
 

time: 126 us -> 124 us (0.984)
  Pallas kernels: 126 us -> 123 us
    pallas_call x1, Pallas kernels: 4.41 us -> 2.83 us  [per_device(): pl.pallas_call(restack, out_shape=jax.ShapeDtypeStruct((256, 64, 128), BF...]
where the time goes in v6:
time: 124 us; the launch traced here: 123 us
  Pallas kernels  123 us (99%)
    pallas_call x1, Pallas kernels, per_device(): pl.pallas_call(kernel, out_shape=pltpu.VMEM((64, 256, 128), BF), in_specs...  120 us
    pallas_call x1, Pallas kernels, per_device(): pl.pallas_call(restack, out_shape=jax.ShapeDtypeStruct((256, 64, 128), BF...  2.83 us

profile of v6, /device:TPU:0, one launch (start us, length us, event | category | flops | bytes accessed | tf_op | source)
XLA Modules:
  0.0 123.1 jit_solution(18395967893022585637)
XLA Ops:
  0.0 120.3 %contract.1.source = bf16[64,256,128]{2,1,0:T(8,128)(2,1)S(1)} custom-call(bf16[16,2048]{1,0:T(8,128)(2,1)} %gv.1, bf16[16,2048]{1,0:T(8,128)(2,1)} %go.1, s32[64]{0:T(128)} %order.1, s32[1,64]{1,0:T(1,128)} %bitcast.1, s32[64,64]{1,0:T(8,128)} %pattern.1, bf16[8,128,2048]{2,1,0:T(8,128)(2,1)} %t_hbm.1), custom_call_target="tpu_custom_call" | custom-call | tf_op jit(solution)/shard_map/contract/pallas_call | solution.py:563
  120.3 2.8 %restack.1 = bf16[256,64,128]{2,1,0:T(8,128)(2,1)} custom-call(bf16[64,256,128]{2,1,0:T(8,128)(2,1)S(1)} %contract.1.source), custom_call_target="tpu_custom_call" | custom-call | tf_op jit(solution)/shard_map/restack/pallas_call | solution.py:589

commit v7 on v6

--- a/solution.py
+++ b/solution.py
@@ -10,7 +10,7 @@
 F32 = jnp.float32
 NC = 4
 ORDERS = ("zyx", "zxy")
-TS, V1, V2, VY, VX, O1, O2, O3, O4, HC, HD, HP, SC, SD, SP = range(15)
+TS, V1, V2, VY, VX, O1, O2, O3, O4, HC, HD, HP, SC, SD, SP = 0, 1, 2, 3, 3, 1, 2, 3, 0, 4, 5, 5, 4, 5, 5
 FAR_ORDER = (1, 3, 2, 0)
 
 
@@ -98,7 +98,10 @@
         for t in range(4):
             turned[t, b] = pltpu.roll(source, t * 32, 1) if t else source
 
-    def permute(j, carry):
+    def permute(i, carry):
+        part = 1 - i // 8
+        core, pair = lax.rem(i, 2), lax.rem(i // 2, 4)
+        j = pair * 4 + part * 2 + core
         wanted = jnp.zeros((16, 128), jnp.int32)
         for s in range(4):
             wanted = jnp.where(lane_slot == s, order[4 * j + s], wanted)
@@ -107,18 +110,20 @@
             first_atom = wanted - lax.rem(lane_slot - t + 4, 4)
             for b in range(16):
                 block = jnp.where(first_atom == 4 * b, turned[t, b], block)
-        gp[lax.rem(j, 2), lax.rem(j // 2, 2), j // 4] = block.astype(BF)
-        return carry
-
-    lax.fori_loop(0, 16, permute, 0)
+        gp[core, part, pair] = block.astype(BF)
+        return carry
+
+    lax.fori_loop(0, 8, permute, 0)
 
     def rows16(core):
         return pl.ds(pl.multiple_of(core * 16, 16), 16)
 
-    own = pltpu.make_async_copy(gp.at[k], gvb.at[:, :, zl, x, y, zh, rows16(k)], own_sem.at[0])
-    own.start()
+    def own(part):
+        return pltpu.make_async_copy(gp.at[k, part], gvb.at[part, :, zl, x, y, zh, rows16(k)], own_sem.at[part])
+
+    own(1).start()
     own_o = pltpu.make_async_copy(
-        go.at[:, pl.ds(pl.multiple_of(k * 1024, 1024), 1024)], gst.at[y * 2 + k], own_sem.at[1]
+        go.at[:, pl.ds(pl.multiple_of(k * 1024, 1024), 1024)], gst.at[y * 2 + k], own_sem.at[2]
     )
     own_o.start()
 
@@ -131,9 +136,12 @@
         )
 
     v1_targets = [(0, 1)] + [(d, e) for d in (1, 3, 2) for e in (0, 1)]
-    for part in (1, 0):
-        for d, e in v1_targets:
-            v1(part, d, e).start()
+    for d, e in v1_targets:
+        v1(1, d, e).start()
+    lax.fori_loop(8, 16, permute, 0)
+    own(0).start()
+    for d, e in v1_targets:
+        v1(0, d, e).start()
 
     def o1(d, e, mine):
         to = moved(p, y=d, k=e)
@@ -196,8 +204,8 @@
     def v2_in(part, j):
         arrived(gst.at[pl.ds(0, 3)], v2r.at[part, j])
 
-    own.wait()
     for part in (1, 0):
+        own(part).wait()
         arrived(turned.at[0, pl.ds(0, 14)], v1r.at[part])
         for j in range(3):
             v2_out(part, j)
@@ -244,19 +252,31 @@
             arrived(hs.at[0, pl.ds(0, 2)], o3r.at[i, 0])
         for side in (0, 1):
             copy(i, side, 2, True).start()
+        if copy is o3:
+            o4(i, False)
 
     def rest_in(copy, i):
         if copy is vx:
             arrived(hs.at[0, pl.ds(0, 2)], vxr.at[i, 1])
         else:
             arrived(hs.at[0, pl.ds(0, 4)], o3r.at[i, 1])
+            o4(i, True)
 
     def vy_in(s):
         arrived(hs.at[0, pl.ds(0, 3)], vyr.at[s])
 
-    def o4(t, mine):
-        slot = got.at[:, :, :, k if mine else 1 - k, :, t]
-        return remote(slot, slot, sent.at[O4], o4r.at[t], moved(p, k=1))
+    def o4(t, last):
+        before, after = moved(p, x=-1)["x"], moved(p, x=1)["x"]
+        every = slice(None)
+        first, second = (0, before), (1, after)
+        if last:
+            first, second = (1, before), (0, after)
+        for half, at in (first, second, (every, moved(p, x=2)["x"] if last else x)):
+            slot = got.at[half, at, :, k, :, t]
+            remote(slot, slot, sent.at[O4], o4r.at[t], moved(p, k=1)).start()
+
+    def o4_in(t):
+        arrived(got.at[:, :, :, 0, :, 0], o4r.at[t])
 
     v2_in(1, 0)
     vy(0, FAR_ORDER[0], True).start()
@@ -296,16 +316,17 @@
         if isinstance(s, int) and s == 0:
             dst, sem = hr.at[c, :, y * 2 + (zh if mine else 1 - zh)], hrr.at[stage(c)]
         else:
-            dst, sem = hz.at[c, s - 1], hur.at[c, s]
+            dst, sem = hz.at[c, s - 1], hur.at[stage(c), s]
         return remote(hs.at[c, lax.rem(y + s, 4) * 2 + 1 - zh], dst, sent.at[HC], sem, moved(p, z=2))
 
     def h_pass(c, s, mine):
         source = moved(p, y=0 if mine else -s)["y"] * 2 + 1 - zh
         return remote(hz.at[c, s - 1], hr.at[c, :, source], sent.at[HP], hrr.at[stage(c)], moved(p, y=s))
 
-    def h_on(c, s):
-        h_cross(c, s, False).wait_recv()
-        h_pass(c, s, True).start()
+    def h_on(chunks, s):
+        arrived(hz.at[0, pl.ds(0, len(chunks))], hur.at[stage(chunks[0]), s])
+        for c in chunks:
+            h_pass(c, s, True).start()
 
     def first(c0, chunks, n):
         pair = lax.rem(y + turn(n), 4)
@@ -348,15 +369,13 @@
     def first_late(n, carry):
         @pl.when(n == 1)
         def _():
-            h_on(0, 1)
-            h_on(1, 1)
+            h_on((0, 1), 1)
             pass_on(o3, 0)
             own_out(o3, 2)
 
         @pl.when(n == 3)
         def _():
-            h_on(0, 3)
-            h_on(1, 3)
+            h_on((0, 1), 3)
 
         first(2, 2, n)
         h_cross(2, turn(n), True).start()
@@ -372,17 +391,14 @@
         h_cross(3, s, True).start()
     pass_on(o3, 1)
     own_out(o3, 3)
-    h_on(0, 2)
-    h_on(1, 2)
+    h_on((0, 1), 2)
     for s in (1, 3, 2):
         h_side(2, s, True).start()
     rest_in(o3, 0)
-    o4(0, True).start()
     pass_on(o3, 2)
-    h_on(2, 1)
+    h_on((2,), 1)
     rest_in(o3, 1)
-    o4(1, True).start()
-    h_on(2, 3)
+    h_on((2,), 3)
     pass_on(o3, 3)
 
     whole = pl.ds(0, 256)
@@ -390,12 +406,16 @@
     def s_slot(c, at, rows):
         return out.at[pl.ds((lax.rem(at["z"], 2) * 4 + at["x"]) * 8 + c * 2, 2), rows]
 
+    def s_straight(c, rows):
+        return remote(ss.at[c, x, 1, :, rows], s_slot(c, p, rows), sent.at[SC], srr.at[0], flip(p, "z"))
+
     def s_out(c, d, rows, part):
         block = ss.at[c, lax.rem(x + d, 4)]
 
         def stay():
             pltpu.make_async_copy(block.at[0, :, rows], s_slot(c, p, rows), srr.at[0]).start()
-            remote(block.at[1, :, rows], s_slot(c, p, rows), sent.at[SC], srr.at[0], flip(p, "z")).start()
+            if isinstance(d, int):
+                s_straight(c, rows).start()
 
         def leave():
             s_cross(c, d, rows, part).start()
@@ -409,19 +429,19 @@
 
     def s_cross(c, d, rows, part):
         return remote(
-            ss.at[c, lax.rem(x + d, 4), 1, :, rows], sz.at[c, d - 1, :, rows], sent.at[SC], zr.at[part, c, d], flip(p, "z")
+            ss.at[c, lax.rem(x + d, 4), 1, :, rows], sz.at[c, d - 1, :, rows], sent.at[SC], zr.at[part, d], flip(p, "z")
         )
 
-    def s_on(c, d, rows, part):
-        s_cross(c, d, rows, part).wait_recv()
-        remote(
-            sz.at[c, d - 1, :, rows], s_slot(c, flip(p, "z"), rows), sent.at[SP], srr.at[0], moved(p, x=d)
-        ).start()
+    def s_on(chunks, d, rows, part):
+        arrived(sz.at[0, 0], zr.at[part, d])
+        for c in chunks:
+            remote(
+                sz.at[c, d - 1, :, rows], s_slot(c, flip(p, "z"), rows), sent.at[SP], srr.at[0], moved(p, x=d)
+            ).start()
 
     def s_on_early(part):
         for i in range(3):
-            for c in (0, 1):
-                s_on(c, far_first(i), pl.ds(part * 128, 128), part)
+            s_on((0, 1), far_first(i), pl.ds(part * 128, 128), part)
 
     def lined_up(c, q):
         rows = []
@@ -453,20 +473,18 @@
     def second_early(t, carry):
         @pl.when(t == 2)
         def _():
-            h_on(2, 2)
+            h_on((2,), 2)
             for s in (1, 3, 2):
                 h_side(3, s, True).start()
-            h_on(3, 1)
+            h_on((3,), 1)
             rest_in(o3, 2)
-            o4(2, True).start()
 
         @pl.when(t == 3)
         def _():
             rest_in(o3, 3)
-            o4(3, True).start()
-            h_on(3, 3)
-
-        o4(t, False).wait_recv()
+            h_on((3,), 3)
+
+        o4_in(t)
         r = second((0, 1), lambda ref: ref[:, t])
         rows = pl.ds(pl.multiple_of(t * 64, 64), 64)
         for c in (0, 1):
@@ -487,7 +505,7 @@
         return carry
 
     lax.fori_loop(0, 4, second_early, 0)
-    h_on(3, 2)
+    h_on((3,), 2)
 
     def second_late(c, carry):
         arrived(hr.at[c], hrr.at[c - 1])
@@ -499,32 +517,33 @@
             for e in (0, 1):
                 for q in range(2):
                     ss[c, owner, e, q] = r[e * 256:(e + 1) * 256, q * 128:(q + 1) * 128]
-            s_out(c, d, whole, 0)
+            s_out(c, d, whole, c)
             return inner
 
         lax.fori_loop(0, 4, tile, 0)
+
+        @pl.when(c == 3)
+        def _():
+            s_straight(2, whole).start()
+            s_straight(3, whole).start()
+
         s_on_early(c - 2)
         return carry
 
     lax.fori_loop(2, 4, second_late, 0)
 
     def s_on_late(i, carry):
-        s_on(2 + i // 3, far_first(lax.rem(i, 3)), whole, 0)
+        s_on((2 + i // 3,), far_first(lax.rem(i, 3)), whole, 2 + i // 3)
         return carry
 
     lax.fori_loop(0, 6, s_on_late, 0)
 
     arrived(out, srr.at[0])
-    arrived(t2.at[:, 0], sent.at[TS])
-    for kind, ref in (
-        (V1, gst.at[pl.ds(0, 7)]), (O1, gst.at[pl.ds(0, 7)]),
-        (V2, got.at[0, pl.ds(0, 3), 0, 0]), (O2, got.at[0, pl.ds(0, 3), 0, 0]),
-        (VY, got.at[0, pl.ds(0, 3), :, 0]), (VX, got.at[0, pl.ds(0, 3), :, 0]),
-        (O3, got.at[0, pl.ds(0, 3)]), (O4, got.at[0]),
-        (HC, got.at[0, pl.ds(0, 2)]), (HD, got.at[0, pl.ds(0, 3), :, 0]), (HP, got.at[0, pl.ds(0, 3), :, 0]),
-        (SC, got.at[0, pl.ds(0, 2)]), (SD, got.at[0, pl.ds(0, 3), :, 0]), (SP, got.at[0, pl.ds(0, 3), :, 0]),
+    for sem, ref in (
+        (TS, t2), (V1, t2.at[0, 0, pl.ds(0, 112)]), (V2, t2.at[pl.ds(0, 3), 0]),
+        (VX, t2.at[pl.ds(0, 6)]), (HC, t2.at[:, 0]), (HD, t2.at[pl.ds(0, 6)]),
     ):
-        arrived(ref, sent.at[kind])
+        arrived(ref, sent.at[sem])
 
 
 def restack(source, out, target, out_sem):
@@ -578,8 +597,8 @@
             pltpu.VMEM((2, 4, 2, 2, 4, 4, 64, 128), BF),
             pltpu.VMEM((NC, 4, 2, 2, 256, 128), BF),
             pltpu.VMEM((NC, 3, 2, 256, 128), BF),
-            dma((NC,)), dma((2,)), dma((15,)), dma((1,)), dma((2,)), dma((2, 4)), dma((4,)), dma((4, 2)),
-            dma((1,)), dma((1,)), dma((4, 2)), dma((4,)), dma((NC, 4)), dma((3,)), dma((2, NC, 4)), dma((1,)),
+            dma((NC,)), dma((3,)), dma((6,)), dma((1,)), dma((2,)), dma((2, 4)), dma((4,)), dma((4, 2)),
+            dma((1,)), dma((1,)), dma((4, 2)), dma((4,)), dma((3, 4)), dma((3,)), dma((4, 4)), dma((1,)),
         ],
         compiler_params=pltpu.CompilerParams(
             collective_id=0, has_side_effects=True, vmem_limit_bytes=56 * 2**20

time: 124 us -> 121 us (0.976)
  Pallas kernels: 123 us -> 121 us
    pallas_call x1, Pallas kernels: 120 us -> 118 us  [per_device(): pl.pallas_call(kernel, out_shape=pltpu.VMEM((64, 256, 128), BF), in_specs...]
where the time goes in v7:
time: 121 us
  Pallas kernels  121 us (100%)
    pallas_call x1, Pallas kernels, per_device(): pl.pallas_call(kernel, out_shape=pltpu.VMEM((64, 256, 128), BF), in_specs...  118 us
    pallas_call x1, Pallas kernels, per_device(): pl.pallas_call(restack, out_shape=jax.ShapeDtypeStruct((256, 64, 128), BF...  2.83 us

profile of v7, /device:TPU:0, one launch (start us, length us, event | category | flops | bytes accessed | tf_op | source)
XLA Modules:
  0.0 120.8 jit_solution(5766764009883330485)
XLA Ops:
  0.0 118.0 %contract.1.source = bf16[64,256,128]{2,1,0:T(8,128)(2,1)S(1)} custom-call(bf16[16,2048]{1,0:T(8,128)(2,1)} %gv.1, bf16[16,2048]{1,0:T(8,128)(2,1)} %go.1, s32[64]{0:T(128)} %order.1, s32[1,64]{1,0:T(1,128)} %bitcast.1, s32[64,64]{1,0:T(8,128)} %pattern.1, bf16[8,128,2048]{2,1,0:T(8,128)(2,1)} %t_hbm.1), custom_call_target="tpu_custom_call" | custom-call | tf_op jit(solution)/shard_map/contract/pallas_call | solution.py:582
  118.0 2.8 %restack.1 = bf16[256,64,128]{2,1,0:T(8,128)(2,1)} custom-call(bf16[64,256,128]{2,1,0:T(8,128)(2,1)S(1)} %contract.1.source), custom_call_target="tpu_custom_call" | custom-call | tf_op jit(solution)/shard_map/restack/pallas_call | solution.py:608

commit v8 on v7

--- a/solution.py
+++ b/solution.py
@@ -11,7 +11,8 @@
 NC = 4
 ORDERS = ("zyx", "zxy")
 TS, V1, V2, VY, VX, O1, O2, O3, O4, HC, HD, HP, SC, SD, SP = 0, 1, 2, 3, 3, 1, 2, 3, 0, 4, 5, 5, 4, 5, 5
-FAR_ORDER = (1, 3, 2, 0)
+EARLY_ROWS = ((0, 128), (128, 64), (192, 64))
+FAR_ORDER = (None, None, 2, 0)
 
 
 def me():
@@ -188,18 +189,21 @@
 
     lax.fori_loop(0, NC, filter_chunk, 0)
 
-    def v2(part, j, d, mine):
+    def v2(part, j, d):
         axis = ORDERS[part][1]
-        at = p if mine else moved(p, **{axis: -d})
         if part == 0:
-            slot = gvb.at[0, lax.rem((y + d if mine else y) + turn(j), 4), :, x, at["y"], :]
+            slots = [gvb.at[0, lax.rem(y + d + turn(j), 4), :, x, y, :]]
+        elif j < 2:
+            slots = [gvb.at[1, lax.rem(y + near, 4), j, x, y, :] for near in (1, 3)]
         else:
-            slot = gvb.at[1, lax.rem(y + FAR_ORDER[j], 4), :, at["x"], y, :]
-        return remote(slot, slot, sent.at[V2], v2r.at[part, j], moved(p, **{axis: d}))
+            slots = [gvb.at[1, lax.rem(y + FAR_ORDER[j], 4), :, x, y, :]]
+        to = moved(p, **{axis: d})
+        return [remote(slot, slot, sent.at[V2], v2r.at[part, j], to) for slot in slots]
 
     def v2_out(part, j):
         for d in (1, 3, 2):
-            v2(part, j, d, True).start()
+            for copy in v2(part, j, d):
+                copy.start()
 
     def v2_in(part, j):
         arrived(gst.at[pl.ds(0, 3)], v2r.at[part, j])
@@ -222,23 +226,30 @@
     for d in (1, 3, 2):
         o2(d, True).start()
 
-    def vy(s, d, mine):
-        pair = lax.rem((y + d if mine else y) + turn(s), 4)
-        slot = gvb.at[1, pair, :, :, y if mine else moved(p, y=-d)["y"], :]
+    def vy(s, d, half=slice(None)):
+        slot = gvb.at[1, lax.rem(y + d + turn(s), 4), half, :, y, :]
         return remote(slot, slot, sent.at[VY], vyr.at[s], moved(p, y=d))
 
     def along_x(ref_of, send, recv, side, n, mine):
         step = 1 - 2 * side
         origin = (x if n < 2 else moved(p, x=-step)["x"]) if mine else moved(p, x=-step if n < 2 else 2)["x"]
         slot = ref_of(side if n == 2 else n, origin)
-        return remote(slot, slot, send, recv.at[0 if n == side else 1], moved(p, x=step))
+        return remote(slot, slot, send, recv[0 if n == side else 1], moved(p, x=step))
 
     def vx(s, side, n, mine):
         pair = lax.rem(y + turn(s), 4)
-        return along_x(lambda half, at: gvb.at[0, pair, half, at], sent.at[VX], vxr.at[s], side, n, mine)
+        return along_x(
+            lambda half, at: gvb.at[0, pair, half, at], sent.at[VX], (vxr.at[s, 0], vxr.at[s, 1]), side, n, mine
+        )
+
+    def vx_first(q, side, n):
+        return along_x(
+            lambda half, at: gvb.at[0, y, half, at, pl.ds(q * 2, 2)],
+            sent.at[VX], (vxr.at[4, q], vxr.at[0, 1]), side, n, True,
+        )
 
     def o3(t, side, n, mine):
-        return along_x(lambda half, at: got.at[half, at, :, k, :, t], sent.at[O3], o3r.at[t], side, n, mine)
+        return along_x(lambda half, at: got.at[half, at, :, k, :, t], sent.at[O3], (o3r.at[t, 0], o3r.at[t, 1]), side, n, mine)
 
     def own_out(copy, i):
         for n in (0, 1):
@@ -279,26 +290,35 @@
         arrived(got.at[:, :, :, 0, :, 0], o4r.at[t])
 
     v2_in(1, 0)
-    vy(0, FAR_ORDER[0], True).start()
+    for d in (1, 3):
+        vy(0, d, 0).start()
     v2_in(0, 0)
-    own_out(vx, 0)
-    for j in (1, 2):
-        v2_in(1, j)
-        vy(0, FAR_ORDER[j], True).start()
+    for other in (0, 1):
+        for q in (0, 1):
+            for side in (0, 1):
+                vx_first(q, side, 1 - side if other else side).start()
+    v2_in(1, 1)
+    for d in (1, 3):
+        vy(0, d, 1).start()
+    v2_in(1, 2)
+    vy(0, 2).start()
     v2_out(1, 3)
     v2_out(0, 3)
-    vy(1, 1, True).start()
-    vy(1, 2, True).start()
+    vy(1, 1).start()
+    vy(1, 2).start()
     v2_in(0, 1)
-    pass_on(vx, 0)
+    for q in (0, 1):
+        arrived(hs.at[0, 0, 0], vxr.at[4, q])
+        for side in (0, 1):
+            vx_first(q, side, 2).start()
     own_out(vx, 1)
     v2_in(0, 2)
     own_out(vx, 2)
     v2_in(1, 3)
-    vy(1, 3, True).start()
+    vy(1, 3).start()
     for s in (2, 3):
         for d in (1, 3, 2):
-            vy(s, d, True).start()
+            vy(s, d).start()
 
     arrived(t2.at[:, 0], tr.at[0])
 
@@ -338,6 +358,12 @@
                 hs[c0 + m, pair * 2 + q] = h[m * 512:(m + 1) * 512, q * 128:(q + 1) * 128].reshape(2, 256, 128)
 
     def first_own(c, carry):
+        @pl.when(c == 2)
+        def _():
+            pass_on(vx, 1)
+            v2_in(0, 3)
+            own_out(vx, 3)
+
         first(c, 1, 0)
         h_cross(c, 0, True).start()
         h_own(c).start()
@@ -346,9 +372,6 @@
     def first_early(n, carry):
         @pl.when(n == 1)
         def _():
-            pass_on(vx, 1)
-            v2_in(0, 3)
-            own_out(vx, 3)
             pass_on(vx, 2)
 
         @pl.when(n == 2)
@@ -433,7 +456,7 @@
         )
 
     def s_on(chunks, d, rows, part):
-        arrived(sz.at[0, 0], zr.at[part, d])
+        arrived(sz.at[pl.ds(0, len(chunks)), 0, :, rows], zr.at[part, d])
         for c in chunks:
             remote(
                 sz.at[c, d - 1, :, rows], s_slot(c, flip(p, "z"), rows), sent.at[SP], srr.at[0], moved(p, x=d)
@@ -441,7 +464,7 @@
 
     def s_on_early(part):
         for i in range(3):
-            s_on((0, 1), far_first(i), pl.ds(part * 128, 128), part)
+            s_on((0, 1), far_first(i), pl.ds(*EARLY_ROWS[part]), part)
 
     def lined_up(c, q):
         rows = []
@@ -494,13 +517,13 @@
                     for q in range(2):
                         ss[c, owner, e, q, rows] = r[at:at + 64, (c * 2 + q) * 128:(c * 2 + q + 1) * 128]
 
-        for part in (0, 1):
-
-            @pl.when(t == part * 2 + 1)
+        for part, (start, size) in enumerate(EARLY_ROWS):
+
+            @pl.when(t == part + 1)
             def _():
                 for i in range(4):
                     for c in (0, 1):
-                        s_out(c, far_first(i), pl.ds(part * 128, 128), part)
+                        s_out(c, far_first(i), pl.ds(start, size), part)
 
         return carry
 
@@ -517,7 +540,7 @@
             for e in (0, 1):
                 for q in range(2):
                     ss[c, owner, e, q] = r[e * 256:(e + 1) * 256, q * 128:(q + 1) * 128]
-            s_out(c, d, whole, c)
+            s_out(c, d, whole, c + 1)
             return inner
 
         lax.fori_loop(0, 4, tile, 0)
@@ -527,13 +550,21 @@
             s_straight(2, whole).start()
             s_straight(3, whole).start()
 
-        s_on_early(c - 2)
+        @pl.when(c == 2)
+        def _():
+            s_on_early(0)
+
+        @pl.when(c == 3)
+        def _():
+            s_on_early(1)
+            s_on_early(2)
+
         return carry
 
     lax.fori_loop(2, 4, second_late, 0)
 
     def s_on_late(i, carry):
-        s_on((2 + i // 3,), far_first(lax.rem(i, 3)), whole, 2 + i // 3)
+        s_on((2 + i // 3,), far_first(lax.rem(i, 3)), whole, 3 + i // 3)
         return carry
 
     lax.fori_loop(0, 6, s_on_late, 0)
@@ -549,30 +580,24 @@
 def restack(source, out, target, out_sem):
     parts = out_sem.shape[0]
     lams = out.shape[0] // parts
-
-    def store(i):
-        some = pl.ds(i * lams, lams)
-        return pltpu.make_async_copy(target.at[some], out.at[some], out_sem.at[i])
-
     to = lax.broadcasted_iota(jnp.int32, (256, 256), 0)
     frm = lax.broadcasted_iota(jnp.int32, (256, 256), 1)
     one_hot = ((to // 16 == lax.rem(frm, 16)) & (lax.rem(to, 16) == frm // 16)).astype(BF)
-
-    def part(i, carry):
-        for pair in range(lams // 32):
+    stores = []
+    for i in range(parts):
+        for base in range(i * lams, (i + 1) * lams, 32):
+            at = [slice(base + h * 16, base + h * 16 + 16) for h in range(2)]
             for group in range(source.shape[0] // 16):
                 ps = slice(group * 16, group * 16 + 16)
-                at = [pl.ds(pl.multiple_of(i * lams + pair * 32 + h * 16, 16), 16) for h in range(2)]
                 rows = jnp.concatenate([source[ps, at[h], :].reshape(256, 128) for h in range(2)], axis=1)
                 moved_rows = jnp.dot(one_hot, rows, preferred_element_type=F32).astype(BF)
                 for h in range(2):
                     target[at[h], ps, :] = moved_rows[:, h * 128:(h + 1) * 128].reshape(16, 16, 128)
-        store(i).start()
-        return carry
-
-    lax.fori_loop(0, parts, part, 0)
-    for i in range(parts):
-        store(i).wait()
+        some = pl.ds(i * lams, lams)
+        stores.append(pltpu.make_async_copy(target.at[some], out.at[some], out_sem.at[i]))
+        stores[-1].start()
+    for store in stores:
+        store.wait()
 
 
 def per_device(three_centre, green_virt, green_occ, pattern, block_sizes, atom_order):
@@ -597,8 +622,8 @@
             pltpu.VMEM((2, 4, 2, 2, 4, 4, 64, 128), BF),
             pltpu.VMEM((NC, 4, 2, 2, 256, 128), BF),
             pltpu.VMEM((NC, 3, 2, 256, 128), BF),
-            dma((NC,)), dma((3,)), dma((6,)), dma((1,)), dma((2,)), dma((2, 4)), dma((4,)), dma((4, 2)),
-            dma((1,)), dma((1,)), dma((4, 2)), dma((4,)), dma((3, 4)), dma((3,)), dma((4, 4)), dma((1,)),
+            dma((NC,)), dma((3,)), dma((6,)), dma((1,)), dma((2,)), dma((2, 4)), dma((4,)), dma((5, 2)),
+            dma((1,)), dma((1,)), dma((4, 2)), dma((4,)), dma((3, 4)), dma((3,)), dma((5, 4)), dma((1,)),
         ],
         compiler_params=pltpu.CompilerParams(
             collective_id=0, has_side_effects=True, vmem_limit_bytes=56 * 2**20
@@ -610,7 +635,7 @@
         out_shape=jax.ShapeDtypeStruct((256, 64, 128), BF),
         in_specs=[vmem],
         out_specs=anywhere,
-        scratch_shapes=[pltpu.VMEM((256, 64, 128), BF), dma((2,))],
+        scratch_shapes=[pltpu.VMEM((256, 64, 128), BF), dma((4,))],
         compiler_params=pltpu.CompilerParams(vmem_limit_bytes=40 * 2**20),
         name="restack",
     )(blocks)

time: 121 us -> 121 us (level)
  no operation moved by 1% of the time
where the time goes in v8:
time: 121 us; the launch traced here: 120 us
  Pallas kernels  120 us (99%)
    pallas_call x1, Pallas kernels, per_device(): pl.pallas_call(kernel, out_shape=pltpu.VMEM((64, 256, 128), BF), in_specs...  118 us
    pallas_call x1, Pallas kernels, per_device(): pl.pallas_call(restack, out_shape=jax.ShapeDtypeStruct((256, 64, 128), BF...  2.48 us

profile of v8, /device:TPU:0, one launch (start us, length us, event | category | flops | bytes accessed | tf_op | source)
XLA Modules:
  0.0 120.4 jit_solution(13227655633231228317)
XLA Ops:
  0.0 118.0 %contract.1.source = bf16[64,256,128]{2,1,0:T(8,128)(2,1)S(1)} custom-call(bf16[16,2048]{1,0:T(8,128)(2,1)} %gv.1, bf16[16,2048]{1,0:T(8,128)(2,1)} %go.1, s32[64]{0:T(128)} %order.1, s32[1,64]{1,0:T(1,128)} %bitcast.1, s32[64,64]{1,0:T(8,128)} %pattern.1, bf16[8,128,2048]{2,1,0:T(8,128)(2,1)} %t_hbm.1), custom_call_target="tpu_custom_call" | custom-call | tf_op jit(solution)/shard_map/contract/pallas_call | solution.py:607
  118.0 2.5 %restack.1 = bf16[256,64,128]{2,1,0:T(8,128)(2,1)} custom-call(bf16[64,256,128]{2,1,0:T(8,128)(2,1)S(1)} %contract.1.source), custom_call_target="tpu_custom_call" | custom-call | tf_op jit(solution)/shard_map/restack/pallas_call | solution.py:633

commit v9 on v8

--- a/solution.py
+++ b/solution.py
@@ -223,7 +223,7 @@
         slot = got.at[lax.rem(at["z"], 2), x, at["z"] // 2, k]
         return remote(slot, slot, sent.at[O2], o2r.at[0], moved(p, z=d))
 
-    for d in (1, 3, 2):
+    for d in (2, 1, 3):
         o2(d, True).start()
 
     def vy(s, d, half=slice(None)):

time: 121 us -> 121 us (level)
  no operation moved by 1% of the time
where the time goes in v9:
time: 121 us; the launch traced here: 120 us
  Pallas kernels  120 us (99%)
    pallas_call x1, Pallas kernels, per_device(): pl.pallas_call(kernel, out_shape=pltpu.VMEM((64, 256, 128), BF), in_specs...  118 us
    pallas_call x1, Pallas kernels, per_device(): pl.pallas_call(restack, out_shape=jax.ShapeDtypeStruct((256, 64, 128), BF...  2.48 us

profile of v9, /device:TPU:0, one launch (start us, length us, event | category | flops | bytes accessed | tf_op | source)
XLA Modules:
  0.0 120.4 jit_solution(11184101818547352762)
XLA Ops:
  0.0 118.0 %contract.1.source = bf16[64,256,128]{2,1,0:T(8,128)(2,1)S(1)} custom-call(bf16[16,2048]{1,0:T(8,128)(2,1)} %gv.1, bf16[16,2048]{1,0:T(8,128)(2,1)} %go.1, s32[64]{0:T(128)} %order.1, s32[1,64]{1,0:T(1,128)} %bitcast.1, s32[64,64]{1,0:T(8,128)} %pattern.1, bf16[8,128,2048]{2,1,0:T(8,128)(2,1)} %t_hbm.1), custom_call_target="tpu_custom_call" | custom-call | tf_op jit(solution)/shard_map/contract/pallas_call | solution.py:607
  118.0 2.5 %restack.1 = bf16[256,64,128]{2,1,0:T(8,128)(2,1)} custom-call(bf16[64,256,128]{2,1,0:T(8,128)(2,1)S(1)} %contract.1.source), custom_call_target="tpu_custom_call" | custom-call | tf_op jit(solution)/shard_map/restack/pallas_call | solution.py:633
